TPU v7x, 256 devices: a whole 4x4x8 slice. The times are simulated.
256 devices in a mesh: row: 16 (over x, y), col: 16 (over z, core).
Axes of the slice: x: 4, y: 4, z: 8, core: 2. Of those that a mesh axis runs over, the one named last changes fastest.
Arguments:
- kernel: float32 [3, 16, 3, 16, 256, 256], P(None, 'row', None, 'col'), as said below
- pattern: int32 [3, 16, 3, 16], P(None, 'row', None, 'col'), may hold values 0 or 1
- factor_cot: float32 [3, 16, 3, 16, 256, 256], P(None, 'row', None, 'col'), may hold values from -6 to 6
Outputs:
- factor: float32 [3, 16, 3, 16, 256, 256], P(None, 'row', None, 'col')
- grad: float32 [3, 16, 3, 16, 256, 256], P(None, 'row', None, 'col')
Inputs may be any that keep to these rules, and one draw needn't show every extreme that they name: `kernel`: entries of blocks off the diagonal lie within -3 / sqrt(256) to 3 / sqrt(256). Diagonal blocks are 4 times the identity plus a symmetric part whose entries lie within -6 / sqrt(256) to 6 / sqrt(256).
All inputs are finite; a program needn't handle non-finite values. No bound on the sum of `pattern` on one device may be relied on, other than what follows from the above.
Results may differ from a plain program's by a relative error of at most 0.0001.
Values sent between devices are 32-bit elements; how exact they have to be, the bound alone decides.
No kernel may reach another device: no remote copies, remote signals or barrier semaphores. Data moves between devices by JAX's collectives and lax.ppermute only.
A program may use at most 128 MiB of HBM per device.

v0:
```python
import jax
import jax.numpy as jnp
from jax import lax
from jax.experimental import pallas as pl
from jax.experimental.pallas import tpu as pltpu
from jax.sharding import PartitionSpec as P

W = 32
B = 256
N = 16
f32 = jnp.float32
HI = lax.Precision.HIGHEST
SMEM = pl.BlockSpec(memory_space=pltpu.SMEM)
PARAMS = pltpu.CompilerParams(vmem_limit_bytes=60 * 1024 * 1024)


def dot(a, b, dims=((1,), (0,))):
    return lax.dot_general(a, b, (dims, ((), ())), precision=HI, preferred_element_type=f32)


def dot_nt(a, b):
    return dot(a, b, ((1,), (1,)))


def dot_tn(a, b):
    return dot(a, b, ((0,), (0,)))


def base_factor(tiles, sub):
    tiles=list(tiles); out=[None]*8
    for tj in range(8):
        live=range(tj,8)
        C=[{t: jnp.broadcast_to(tiles[t][:, 8*tj+k:8*tj+k+1],(8,128)) for t in live} for k in range(8)]
        R=[jnp.broadcast_to(tiles[tj][k:k+1,:],(8,128)) for k in range(8)]
        s=[[None]*8 for _ in range(8)]
        for k in range(8):
            for i in range(k,8):
                s[i][k]=jnp.broadcast_to(C[k][tj][i:i+1,:],(8,128))
        inv=[None]*8
        for k in range(8):
            inv[k]=1.0/s[k][k]
            for i in range(k+1,8):
                l=s[i][k]*inv[k]
                for m in range(i,8): s[m][i]=s[m][i]-l*s[m][k]
                R[i]=R[i]-l*R[k]
                for t in live:
                    if t>tj: C[i][t]=C[i][t]-l*C[k][t]
        rows=R[0]*lax.rsqrt(s[0][0])
        for k in range(1,8): rows=jnp.where(sub==k,R[k]*lax.rsqrt(s[k][k]),rows)
        out[tj]=rows
        for t in live:
            if t==tj: continue
            upd=(C[0][t]*inv[0])*R[0]
            for k in range(1,8): upd=upd+(C[k][t]*inv[k])*R[k]
            tiles[t]=tiles[t]-upd
    return jnp.concatenate(out,0)


def chol_start(v_ref):
    rows = lax.broadcasted_iota(jnp.int32, (B, B), 0)
    cols = lax.broadcasted_iota(jnp.int32, (B, B), 1)
    v_ref[...] = (rows == cols).astype(f32)


def chol_blocks(a_ref, v_ref, blocks):
    nb = 64
    sub = lax.broadcasted_iota(jnp.int32, (8, 128), 0)
    row = lax.broadcasted_iota(jnp.int32, (nb, nb), 0)
    col = lax.broadcasted_iota(jnp.int32, (nb, nb), 1)
    eye = (row == col).astype(f32)
    for b in blocks:
        lo, hi = b * nb, (b + 1) * nb
        d = jnp.concatenate([a_ref[lo:hi, lo:hi], eye], 1)
        uw = base_factor([d[8 * t : 8 * t + 8] for t in range(8)], sub)
        w = uw[:, nb:]
        vp = dot(w, v_ref[lo:hi, :])
        v_ref[lo:hi, :] = vp
        a_ref[lo:hi, lo:hi] = jnp.where(row <= col, uw[:, :nb], 0.0)
        if hi < B:
            up = dot(w, a_ref[lo:hi, hi:])
            a_ref[lo:hi, hi:] = up
            a_ref[hi:, hi:] = a_ref[hi:, hi:] - dot_tn(up, up)
            v_ref[hi:, :] = v_ref[hi:, :] - dot_tn(up, vp)
        if lo > 0:
            a_ref[lo:hi, :lo] = jnp.zeros((nb, lo), f32)


def whole(x):
    return pl.BlockSpec(x.shape, lambda i: (0,) * len(x.shape), pipeline_mode=pl.Buffered(1))


def run(body, name, outputs, scratch, *args):
    return pl.pallas_call(
        body,
        grid=(1,),
        out_shape=outputs,
        in_specs=[SMEM if x.dtype == jnp.int32 else whole(x) for x in args],
        out_specs=jax.tree.map(whole, outputs),
        scratch_shapes=scratch,
        compiler_params=PARAMS,
        name=name,
    )(*args)


def array(*shape):
    return jax.ShapeDtypeStruct(shape, f32)


def split(x):
    hi = x.astype(jnp.bfloat16)
    return hi, (x - hi.astype(f32)).astype(jnp.bfloat16)


def dot3(a, b, dims=((1,), (0,))):
    def product(x, y):
        return lax.dot_general(x, y, (dims, ((), ())), preferred_element_type=f32)

    return product(a[0], b[0]) + (product(a[0], b[1]) + product(a[1], b[0]))


NT = ((1,), (1,))
TN = ((0,), (0,))


def part_of(pair, rows=slice(None), cols=slice(None)):
    return pair[0][rows, cols], pair[1][rows, cols]


def corner_a_kernel(info, own, far, v_ref, l_ref, p_ref, x_ref, a_ref, k10, k11):
    even = info[1] % 2 == 0
    for q in range(8):
        rows = slice(32 * q, 32 * q + 32)
        a_ref[rows, :] = jnp.where(even, own[q, :32], far[q, :32])
        k10[rows, :] = jnp.where(even, own[q, 32:], far[q, 32:])
        k11[rows, :] = jnp.where(even, far[q, 32:], own[q, 32:])
    chol_start(v_ref)
    chol_blocks(a_ref, v_ref, range(4))
    l_ref[...] = a_ref[...].T
    p = dot_nt(k10[...], v_ref[...])
    p_ref[...] = p
    x_ref[...] = k11[...] - dot_nt(p, p)


def corner_c_kernel(x_ref, a_ref, v_ref):
    a_ref[...] = x_ref[...]
    chol_start(v_ref)
    chol_blocks(a_ref, v_ref, (0, 1))


def corner_d_kernel(a_in, v_in, v0_ref, p_ref, v_ref, l_ref, u_ref, a_ref):
    a_ref[...] = a_in[...]
    v_ref[...] = v_in[...]
    chol_blocks(a_ref, v_ref, (2, 3))
    l_ref[...] = a_ref[...].T
    u_ref[...] = dot_nt(dot_tn(v0_ref[...], p_ref[...].T), v_ref[...])


def corner_call(body, name, outputs, scratch, *args):
    return run(body, name, [array(B, B)] * outputs, [pltpu.VMEM((B, B), f32)] * scratch, *args)


def partial_kernel(info, cot, own, far, cols, ca, co, xi, xj, row_own, row_cross, col_out, row_out):
    row, col = info[0], info[1]
    sr, sc = info[2], info[3]
    mask = info[4].astype(f32)
    p, a = col // 2, col % 2
    for k in range(4):
        for h in range(2):
            at = pl.multiple_of((p ^ (4 * h + k)) * 64, 64)
            source = slice(128 * k + 64 * h, 128 * k + 64 * h + 64)
            xi[a, pl.ds(at, 64), :] = own[source, :]
            xi[1 - a, pl.ds(at, 64), :] = far[source, :]
    for source in range(16):
        q, b = source // 2, source % 2
        xj[b, 64 * q : 64 * q + 64, :] = cols[source, :64, :]
    g00 = split(cot[sr, sc] * mask)
    g10 = split(cot[sr + 1, sc])
    g11 = split(cot[sr + 1, sc + 1] * mask)
    xi_wide = split(jnp.concatenate([xi[0], xi[1]], 1))
    xj_wide = split(jnp.concatenate([xj[0], xj[1]], 1))
    top, low = slice(0, B), slice(B, 2 * B)
    i0, i1 = part_of(xi_wide, top), part_of(xi_wide, low)
    j0, j1 = part_of(xj_wide, top), part_of(xj_wide, low)
    h_row = jnp.concatenate([dot3(g00, j0), dot3(g10, j0) + dot3(g11, j1)], 0)
    h_col = jnp.concatenate([dot3(g00, i0, TN) + dot3(g10, i1, TN), dot3(g11, i1, TN)], 0)
    n = dot3(xi_wide, split(h_row), TN)
    t = n + n.T
    t3 = (t[:B, :B], t[:B, B:], t[B:, B:])
    for q in range(8):
        m = p ^ q
        k, h = m % 4, m // 4
        for b in range(2):
            slot = jnp.where(a == b, 0, 1)
            row_out[slot, k, h, :64, :] = h_row[64 * q : 64 * q + 64, B * b : B * b + B]
            for part in range(3):
                at = 384 * b + 48 * q + 16 * part
                row_out[slot, k, h, 64 + 16 * part : 80 + 16 * part, :] = t3[at // B][at % B : at % B + 16]
    for target in range(16):
        q, b = target // 2, target % 2
        col_out[target, :64, :] = h_col[64 * q : 64 * q + 64, B * b : B * b + B]

    @pl.when(col < 2)
    def _():
        first = a == 0
        e0 = split(jnp.where(first, ca[...], co[...]))
        e1 = split(jnp.where(first, co[...], ca[...]))
        x0, x1 = part_of(xi_wide, cols=top), part_of(xi_wide, cols=low)
        d = jnp.concatenate([dot3(e0, x0, TN), dot3(e1, x0, TN), dot3(e1, x1, TN)], 0)
        half = jnp.where(first, d[:384], d[384:])
        for target in range(16):
            col_out[target, 64:, :] = half[24 * target : 24 * target + 24]

    @pl.when(col >= 2)
    def _():
        col_out[:, 64:, :] = jnp.zeros((16, 24, B), f32)

    row_own[...] = row_out[0]
    row_cross[...] = row_out[1]


def partials(*args):
    outputs = [array(2, 512, B)] * 2 + [array(4, 2, 112, B)] * 2 + [array(16, 88, B)]
    return run(partial_kernel, "partials", outputs, [pltpu.VMEM((2, 4, 2, 112, B), f32)], *args)


def sums_kernel(by_col, near, came, h_row, h_col, td):
    total = by_col[0]
    for m in range(1, 16):
        total = total + by_col[m]
    part = near[...] + came[...]
    h_row[...] = part[:64]
    h_col[...] = total[:64]
    both = jnp.concatenate([part[64:], total[64:]], 0)
    for m in range(16):
        td[m] = both


def sums(*args):
    return run(sums_kernel, "sums", [array(64, B), array(64, B), array(16, 72, B)], [], *args)


def table_kernel(td, h_row, h_col, send, d):
    send[:64, :] = h_row[...] + h_col[...]
    total = td[0, :48, :]
    for m in range(1, 16):
        total = total + td[m, :48, :]
    send[64:, :] = total
    for m in range(16):
        d[24 * m : 24 * m + 24, :] = td[m, 48:, :]


def table_sums(*args):
    return run(table_kernel, "table_sums", [array(112, B), array(384, B)], [], *args)


def joined_kernel(*refs):
    at = 0
    for ref in refs[:-1]:
        refs[-1][at : at + ref.shape[0], :] = ref[...]
        at += ref.shape[0]


def joined(pieces):
    return run(joined_kernel, "joined", array(sum(x.shape[0] for x in pieces), B), [], *pieces)


def factor_kernel(info, kernel, xi, xj, v0, v1, u, p01, l0, l1, out):
    row, col = info[0], info[1]
    sr, sc = info[2], info[3]
    mask = info[4].astype(f32)
    for i in range(3):
        for j in range(3):
            out[i, j] = kernel[i, j] * info[5 + 3 * i + j].astype(f32)
    w0, w1, mix = split(v0[...]), split(v1[...]), split(u[...])

    def panels(x):
        x0, x1 = split(x[0]), split(x[1])
        return dot3(x0, w0, NT), dot3(x1, w1, NT) - dot3(x0, mix)

    i0, i1 = panels(xi)
    j0, j1 = panels(xj)
    pi = split(jnp.concatenate([i0, i1], 1))
    pj = split(jnp.concatenate([j0, j1], 1))
    top, low = slice(0, B), slice(B, 2 * B)
    out[sr, sc] = out[sr, sc] - mask * dot3(part_of(pi, top), part_of(pj, top), NT)
    out[sr + 1, sc] = out[sr + 1, sc] - dot3(part_of(pi, low), part_of(pj, top), NT)
    out[sr + 1, sc + 1] = out[sr + 1, sc + 1] - mask * dot3(part_of(pi, low), part_of(pj, low), NT)

    @pl.when(col < 2)
    def _():
        mine = jnp.where(col == 0, i0, i1)
        zero = jnp.zeros((B, B), f32)
        out[2, 0] = zero
        out[0, 0] = zero
        out[sr, 0] = mine[:B]
        out[sr + 1, 0] = mine[B:]

        @pl.when(row == 0)
        def _():
            out[0, 0] = jnp.where(col == 0, l0[...], zero)

        @pl.when(row == 1)
        def _():
            out[0, 0] = jnp.where(col == 0, p01[...], l1[...])


def factor_of(*args):
    return run(factor_kernel, "factor", array(3, 3, B, B), [], *args)


def pull_cholesky(l, v, bar):
    rows = lax.broadcasted_iota(jnp.int32, (B, B), 0)
    cols = lax.broadcasted_iota(jnp.int32, (B, B), 1)
    inner = dot3(l, split(bar), TN)
    phi = jnp.where(rows > cols, inner, jnp.where(rows == cols, 0.5 * inner, 0.0))
    full = dot3(split(dot3(v, split(phi), TN)), v)
    return 0.5 * (full + full.T)


def grad_kernel(info, cot, mine, other, ca, co, ea, eo, v0, v1, u, p01, l0, l1, out):
    row, col = info[0], info[1]
    sr = info[2]
    for i in range(3):
        for j in range(3):
            out[i, j] = cot[i, j] * info[5 + 3 * i + j].astype(f32)

    @pl.when(col < 2)
    def _():
        first = col == 0
        left = jnp.where(first, mine[...], other[...])
        right = jnp.where(first, other[...], mine[...])
        h0 = jnp.concatenate([left[112 * q : 112 * q + 64] for q in range(8)], 0)
        h1 = jnp.concatenate([right[112 * q : 112 * q + 64] for q in range(8)], 0)
        e0 = jnp.where(first, ca[...], co[...])
        e1 = jnp.where(first, co[...], ca[...])
        w0, w1, mix, p = split(v0[...]), split(v1[...]), split(u[...]), split(p01[...])
        h0s = split(h0)
        bar1 = e1 - dot3(split(h1), w1, NT) + dot3(h0s, mix)
        g1 = dot3(split(bar1), w1)
        g0 = dot3(split(e0 - dot3(h0s, w0, NT) - dot3(split(g1), p)), w0)
        zero = jnp.zeros((B, B), f32)
        column = jnp.where(first, g0, g1)
        out[0, 0] = zero
        out[2, 0] = zero
        out[sr, 0] = column[:B] * cot_keep(info, sr)
        out[sr + 1, 0] = column[B:] * cot_keep(info, sr + 1)

        @pl.when(row < 2)
        def _():
            t = jnp.concatenate([x[112 * q + 64 : 112 * q + 112] for x in (left, right) for q in range(8)], 0)
            d = jnp.concatenate([left[896:], right[896:]], 0)
            t00, t01, t11 = t[:B], t[B : 2 * B], t[2 * B :]
            d00, d10, d11 = d[:B], d[B : 2 * B], d[2 * B :]
            c10 = jnp.where(first, ea[...], eo[...])
            c11 = jnp.where(first, eo[...], ea[...])
            t00s, t01s = split(t00), split(t01)
            a10 = split(d10 - dot3(w1, t01s, NT) + dot3(mix, t00s, TN))
            a11 = split(d11 - dot3(w1, split(t11)) + dot3(mix, t01s, TN))
            s1 = dot3(a11, w1, NT) - dot3(a10, mix)
            b1 = pull_cholesky(split(l1[...]), w1, c11 - dot3(w1, split(s1), TN))
            va = split(dot3(w1, a10, TN))
            bar10 = split(c10 - 2.0 * dot3(split(b1), p) - dot3(va, w0, NT))
            s0 = dot3(split(d00 - dot3(w0, t00s) - dot3(p, va, TN)), w0, NT)
            b0 = pull_cholesky(split(l0[...]), w0, cot[0, 0] - dot3(w0, split(s0 + dot3(bar10, p, TN)), TN))
            upper = jnp.where(first, b0, zero)
            lower = jnp.where(first, dot3(bar10, w0), b1)
            out[0, 0] = jnp.where(row == 0, upper, lower) * cot_keep(info, 0)


def cot_keep(info, slot):
    return info[5 + 3 * slot].astype(f32)


def grad_of(*args):
    return run(grad_kernel, "grad", array(3, 3, B, B), [], *args)


Z_GROUPS = [list(range(0, N, 2)), list(range(1, N, 2))]


def flip(x, axis, m):
    return lax.ppermute(x, axis, [(i, i ^ m) for i in range(N)])


def transposed(x):
    return lax.ppermute(x, ("row", "col"), [(r * N + c, c * N + r) for r in range(N) for c in range(N)])


def after(x, *done):
    return lax.optimization_barrier((x,) + done)[0]


def on_device(kernel, pattern, factor_cot):
    row = lax.axis_index("row")
    col = lax.axis_index("col")
    kernel3 = kernel.reshape(3, 3, B, B)
    cot3 = factor_cot.reshape(3, 3, B, B)
    row_ids = jnp.arange(3, dtype=jnp.int32) * N + row
    col_ids = jnp.arange(3, dtype=jnp.int32) * N + col
    distance = row_ids[:, None] - col_ids[None, :]
    kept = (pattern.reshape(3, 3) == 1) & (distance > 0) & (distance <= W)
    keep = ((distance == 0) | kept).astype(jnp.int32)
    sr = (row < 2).astype(jnp.int32)
    sc = (col < 2).astype(jnp.int32)
    mask = (row + N * sr >= col + N * sc).astype(jnp.int32)
    info = jnp.concatenate([jnp.stack([row, col, sr, sc, mask]), keep.reshape(9)])

    column = kernel3[:, 0] * keep[:, 0].astype(f32)[:, None, None]
    xa = lax.dynamic_slice_in_dim(column, sr, 2, 0).reshape(512, B)
    ca = lax.dynamic_slice_in_dim(cot3[:, 0], sr, 2, 0).reshape(512, B)
    corner_block = jnp.where(row < 2, column[0], 0.0)

    pieces = [
        jnp.concatenate([xa[64 * q : 64 * q + 64], corner_block[32 * q : 32 * q + 32]], 0) for q in range(8)
    ]
    row_piece = jnp.where(col < 2, pieces[0], 0.0)
    for q in range(1, 8):
        row_piece = row_piece + lax.ppermute(pieces[q], "col", [(a, 2 * q + a) for a in range(2)])
    corner_piece = row_piece[64:]
    row_piece = row_piece[:64]

    col_send = jnp.concatenate([transposed(row_piece), corner_piece], 0)
    send = jnp.concatenate([row_piece, flip(row_piece, "col", 8)], 0)
    send, col_send = lax.optimization_barrier((send, col_send))
    cols = lax.all_to_all(jnp.broadcast_to(col_send, (N, 96, B)), "row", 0, 0)
    own = jnp.concatenate([send] + [flip(send, "col", 2 * m) for m in range(1, 4)], 0)
    far = flip(own, "col", 1)
    co = flip(after(ca, own), "col", 1)

    cut = jnp.broadcast_to(cols[:2, 64:].reshape(64, B), (8, 64, B))
    cut = lax.all_to_all(cut, "col", 0, 0, axis_index_groups=Z_GROUPS)

    xi, xj, row_own, row_cross, by_col = partials(info, cot3, own, far, cols, ca, co)

    by_col = lax.all_to_all(by_col, "row", 0, 0)
    crossed = flip(row_cross, "col", 1)
    part = [row_own[k] + crossed[k] for k in range(4)]
    part, cut = lax.optimization_barrier((part, cut))
    cut_far = flip(cut, "col", 1)
    v0, l0, p01, x1 = corner_call(corner_a_kernel, "corner_a", 4, 3, info, cut, cut_far)
    came = [flip(part[m], "col", 2 * m) for m in range(1, 4)]
    edge = cot3[0, 0]
    from_one = lax.ppermute(after(edge, cut_far), "row", [(1, 0)])
    came, x1 = lax.optimization_barrier((came, x1))
    part = part[0] + came[0] + came[1] + came[2]
    near, came = part[0], flip(part[1], "col", 8)
    by_col, came, x1, from_one = lax.optimization_barrier((by_col, came, x1, from_one))
    h_row, h_col, td = sums(by_col, near, came)
    td, x1, h_col = lax.optimization_barrier((td, x1, h_col))
    td = lax.all_to_all(td, "row", 0, 0)
    h_col = transposed(h_col)
    ea = jnp.where(row == 0, from_one, edge)
    eo = flip(ea, "col", 1)
    a1, v1 = corner_call(corner_c_kernel, "corner_c", 2, 0, x1)
    v1, l1, u = corner_call(corner_d_kernel, "corner_d", 3, 1, a1, v1, v0, p01)
    td, u, eo, h_col = lax.optimization_barrier((td, u, eo, h_col))

    send, d_half = table_sums(td, h_row, h_col)
    send, xi = lax.optimization_barrier((send, xi))
    def to_owner(x, q):
        return lax.ppermute(x, "col", [(2 * q + a, a) for a in range(2)])

    pieces = [to_owner(send, q) for q in range(3, 8)]
    factor_out = factor_of(info, kernel3, xi, xj, v0, v1, u, p01, l0, l1)
    again, factor_out = lax.optimization_barrier((send, factor_out))
    pieces = [send] + [to_owner(again, q) for q in range(1, 3)] + pieces
    mine = joined(pieces + [d_half])
    theirs = flip(mine, "col", 1)
    grad_out = grad_of(info, cot3, mine, theirs, ca, co, ea, eo, v0, v1, u, p01, l0, l1)
    return (factor_out.reshape(kernel.shape), grad_out.reshape(kernel.shape))


def solution(mesh):
    spec = P(None, "row", None, "col", None, None)
    return jax.shard_map(
        on_device,
        mesh=mesh,
        in_specs=(spec, P(None, "row", None, "col"), spec),
        out_specs=(spec, spec),
        check_vma=False,
    )
```

profile of v0, /device:TPU:1, one launch (start us, length us, event | category | flops | bytes accessed | tf_op | source)
XLA Modules:
  0.0 220.7 jit_solution(764364247759026112)
XLA Ops:
  0.7 0.7 fusion.16
  1.6 1.3 fusion
  3.0 4.4 %collective-permute-start = (f32[96,256]{1,0:T(8,128)S(1)}, f32[96,256]{1,0:T(8,128)S(1)}, u32[]{:S(2)}, u32[]{:S(2)}) collective-permute-start(f32[96,256]{1,0:T(8,128)S(1)} %pad_maximum_fusion.1), channel_id=1, source_target_pairs={{0,2},{1,3},{16,18},{17,19},{32,34},{33,35},{48,50},{49,51},{64,66... | collective-permute-start | bytes 294920 | tf_op jit(solution)/shard_map/ppermute | solution.py:418
  7.4 2.0 collective-permute-start.1
  9.4 2.0 collective-permute-start.2
  11.5 3.2 %collective-permute-start.3 = (f32[96,256]{1,0:T(8,128)S(1)}, f32[96,256]{1,0:T(8,128)S(1)}, u32[]{:S(2)}, u32[]{:S(2)}) collective-permute-start(f32[96,256]{1,0:T(8,128)S(1)} %pad_maximum_fusion.4), channel_id=1, source_target_pairs={{0,8},{1,9},{16,24},{17,25},{32,40},{33,41},{48,56},{49,57},{64,72... | collective-permute-start | bytes 294920 | tf_op jit(solution)/shard_map/ppermute | solution.py:418
  14.7 1.3 collective-permute-start.4
  16.1 1.3 collective-permute-start.5
  17.4 1.3 collective-permute-start.6
  18.7 1.2 collective-permute-done.5
  20.0 2.1 collective-permute-done.6
  22.3 5.2 %collective-permute-start.8 = (f32[64,256]{1,0:T(8,128)S(1)}, f32[64,256]{1,0:T(8,128)S(1)}, u32[]{:S(2)}, u32[]{:S(2)}) collective-permute-start(f32[64,256]{1,0:T(8,128)S(1)} %slice.190), channel_id=1, source_target_pairs={{0,0},{1,16},{2,32},{3,48},{4,64},{5,80},{6,96},{7,112},{8,128},{9... | collective-permute-start | bytes 196616 | tf_op jit(solution)/shard_map/ppermute | solution.py:386
  27.4 1.8 collective-permute-done.7
  29.4 1.3 broadcast_in_dim.19
  30.7 14.7 %all-to-all-start = ((f32[16,96,256]{2,1,0:T(8,128)}), f32[16,96,256]{2,1,0:T(8,128)S(1)}, u32[]{:S(2)}, u32[]{:S(2)}) async-start(f32[16,96,256]{2,1,0:T(8,128)} %broadcast_in_dim.19), calls=%async_computation | async-start | bytes 3145728 | tf_op jit(solution)/shard_map/all_to_all | solution.py:425
  45.4 1.2 slice.192
  46.8 4.0 %collective-permute-start.11 = (f32[128,256]{1,0:T(8,128)S(1)}, f32[128,256]{1,0:T(8,128)S(1)}, u32[]{:S(2)}, u32[]{:S(2)}) collective-permute-start(f32[128,256]{1,0:T(8,128)S(1)} %pad_maximum_fusion), channel_id=1, source_target_pairs={{0,6},{1,7},{2,4},{3,5},{4,2},{5,3},{6,0},{7,1},{8,14},{9,15},{10,... | collective-permute-start | bytes 393224 | tf_op jit(solution)/shard_map/ppermute | solution.py:382
  51.1 0.7 constant_dynamic-update-slice_fusion.3
  51.8 0.6 constant_dynamic-update-slice_fusion.2
  52.4 9.8 %collective-permute-done.10 = f32[128,256]{1,0:T(8,128)S(1)} collective-permute-done((f32[128,256]{1,0:T(8,128)S(1)}, f32[128,256]{1,0:T(8,128)S(1)}, u32[]{:S(2)}, u32[]{:S(2)}) %collective-permute-start.10) | collective-permute-done | bytes 131104 | tf_op jit(solution)/shard_map/ppermute | solution.py:382
  62.2 0.7 constant_dynamic-update-slice_fusion.1
  62.9 0.7 constant_dynamic-update-slice_fusion.own
  63.6 1.7 collective-permute-start.12
  65.6 0.7 concatenate.36.info
  66.3 0.9 broadcast_in_dim.20
  67.2 6.2 %all-to-all-start.2 = ((f32[8,64,256]{2,1,0:T(8,128)}), f32[8,64,256]{2,1,0:T(8,128)S(1)}, u32[]{:S(2)}, u32[]{:S(2)}) async-start(f32[8,64,256]{2,1,0:T(8,128)} %broadcast_in_dim.20), calls=%async_computation.2 | async-start | bytes 1048576 | tf_op jit(solution)/shard_map/all_to_all | solution.py:431
  73.5 0.8 copy-done.5
  74.3 8.5 %partials.1 = (f32[2,512,256]{2,1,0:T(8,128)}, f32[2,512,256]{2,1,0:T(8,128)}, f32[4,2,112,256]{3,2,1,0:T(8,128)}, f32[4,2,112,256]{3,2,1,0:T(8,128)}, f32[16,88,256]{2,1,0:T(8,128)}) custom-call(s32[14]{0:T(128)} %concatenate.36.info, f32[3,3,256,256]{3,2,1,0:T(8,128)} %bitcast.59, f32[512,256]{1,0:T(8,128)} %constant_dynamic-update-slice_fusion.own, ...), custom_call_target="tpu_custom_call" | custom-call | tf_op jit(solution)/shard_map/partials/pallas_call | solution.py:93
  82.8 3.0 %collective-permute-start.14 = (f32[4,2,112,256]{3,2,1,0:T(8,128)}, f32[4,2,112,256]{3,2,1,0:T(8,128)}, u32[]{:S(2)}, u32[]{:S(2)}) collective-permute-start(f32[4,2,112,256]{3,2,1,0:T(8,128)} %get-tuple-element.54), channel_id=1, source_target_pairs={{0,1},{1,0},{2,3},{3,2},{4,5},{5,4},{6,7},{7,6},{8,9},{9,8},{10,11... | collective-permute-start | bytes 2752520 | tf_op jit(solution)/shard_map/ppermute | solution.py:382
  85.7 2.1 all-to-all-done.2.own
  87.9 5.6 %all-to-all-start.1 = ((f32[16,88,256]{2,1,0:T(8,128)}), f32[16,88,256]{2,1,0:T(8,128)S(1)}, u32[]{:S(2)}, u32[]{:S(2)}) async-start(f32[16,88,256]{2,1,0:T(8,128)} %get-tuple-element.52), calls=%async_computation.1 | async-start | bytes 2883584 | tf_op jit(solution)/shard_map/all_to_all | solution.py:435
  93.5 2.2 fusion.1
  95.6 2.8 %collective-permute-start.18 = (f32[8,64,256]{2,1,0:T(8,128)S(1)}, f32[8,64,256]{2,1,0:T(8,128)S(1)}, u32[]{:S(2)}, u32[]{:S(2)}) collective-permute-start(f32[8,64,256]{2,1,0:T(8,128)S(1)} %all-to-all-done.2.own), channel_id=1, source_target_pairs={{0,1},{1,0},{2,3},{3,2},{4,5},{5,4},{6,7},{7,6},{8,9},{9,8},{10,11... | collective-permute-start | bytes 1572872 | tf_op jit(solution)/shard_map/ppermute | solution.py:382
  98.7 3.3 %collective-permute-start.17 = (f32[2,112,256]{2,1,0:T(8,128)S(1)}, f32[2,112,256]{2,1,0:T(8,128)}, u32[]{:S(2)}, u32[]{:S(2)}) collective-permute-start(f32[2,112,256]{2,1,0:T(8,128)S(1)} %get-tuple-element.58), channel_id=1, source_target_pairs={{0,6},{1,7},{2,4},{3,5},{4,2},{5,3},{6,0},{7,1},{8,14},{9,15},{10,... | collective-permute-start | bytes 688136 | tf_op jit(solution)/shard_map/ppermute | solution.py:382
  102.0 1.0 slice_bitcast_fusion.1
  103.0 1.5 collective-permute-start.20
  104.5 13.6 %corner_a.1 = (f32[256,256]{1,0:T(8,128)}, f32[256,256]{1,0:T(8,128)}, f32[256,256]{1,0:T(8,128)}, f32[256,256]{1,0:T(8,128)}) custom-call(s32[14]{0:T(128)} %concatenate.36.info, f32[8,64,256]{2,1,0:T(8,128)} %copy-done.4, f32[8,64,256]{2,1,0:T(8,128)} %copy-done.9), custom_call_target="tpu_custom_call" | custom-call | tf_op jit(solution)/shard_map/corner_a/pallas_call | solution.py:93
  118.1 1.1 add_add_fusion
  119.2 0.7 slice_bitcast_fusion.2
  120.2 7.3 %collective-permute-done.19.came = f32[112,256]{1,0:T(8,128)S(1)} collective-permute-done((f32[112,256]{1,0:T(8,128)S(1)}, f32[112,256]{1,0:T(8,128)S(1)}, u32[]{:S(2)}, u32[]{:S(2)}) %collective-permute-start.19) | collective-permute-done | bytes 114720 | tf_op jit(solution)/shard_map/ppermute | solution.py:382
  127.5 0.6 copy-done.11
  128.1 2.6 %sums.1 = (f32[64,256]{1,0:T(8,128)}, f32[64,256]{1,0:T(8,128)}, f32[16,72,256]{2,1,0:T(8,128)}) custom-call(f32[16,88,256]{2,1,0:T(8,128)} %copy-done.1, f32[112,256]{1,0:T(8,128)} %get-tuple-element.124.near, f32[112,256]{1,0:T(8,128)} %copy-done.11), custom_call_target="tpu_custom_call" | custom-call | tf_op jit(solution)/shard_map/sums/pallas_call | solution.py:93
  130.7 6.5 %all-to-all-start.3 = ((f32[16,72,256]{2,1,0:T(8,128)}), f32[16,72,256]{2,1,0:T(8,128)S(1)}, u32[]{:S(2)}, u32[]{:S(2)}) async-start(f32[16,72,256]{2,1,0:T(8,128)} %get-tuple-element.71), calls=%async_computation.3 | async-start | bytes 2359296 | tf_op jit(solution)/shard_map/all_to_all | solution.py:450
  137.2 1.0 broadcast_select_fusion.ea
  138.2 2.7 %collective-permute-start.21 = (f32[256,256]{1,0:T(8,128)S(1)}, f32[256,256]{1,0:T(8,128)S(1)}, u32[]{:S(2)}, u32[]{:S(2)}) collective-permute-start(f32[256,256]{1,0:T(8,128)S(1)} %broadcast_select_fusion.ea), channel_id=1, source_target_pairs={{0,1},{1,0},{2,3},{3,2},{4,5},{5,4},{6,7},{7,6},{8,9},{9,8},{10,11... | collective-permute-start | bytes 786440 | tf_op jit(solution)/shard_map/ppermute | solution.py:382
  140.8 14.4 %collective-permute-start.22 = (f32[64,256]{1,0:T(8,128)S(1)}, f32[64,256]{1,0:T(8,128)S(1)}, u32[]{:S(2)}, u32[]{:S(2)}) collective-permute-start(f32[64,256]{1,0:T(8,128)S(1)} %copy-done.21), channel_id=1, source_target_pairs={{0,0},{1,16},{2,32},{3,48},{4,64},{5,80},{6,96},{7,112},{8,128},{9... | collective-permute-start | bytes 196616 | tf_op jit(solution)/shard_map/ppermute | solution.py:386
  155.3 7.2 %corner_c.1 = (f32[256,256]{1,0:T(8,128)}, f32[256,256]{1,0:T(8,128)}) custom-call(f32[256,256]{1,0:T(8,128)} %get-tuple-element.72.x_ref), custom_call_target="tpu_custom_call" | custom-call | tf_op jit(solution)/shard_map/corner_c/pallas_call | solution.py:93
  162.4 7.5 %corner_d.1 = (f32[256,256]{1,0:T(8,128)}, f32[256,256]{1,0:T(8,128)}, f32[256,256]{1,0:T(8,128)}) custom-call(f32[256,256]{1,0:T(8,128)} %get-tuple-element.73.a_in, f32[256,256]{1,0:T(8,128)} %get-tuple-element.74.v_in, f32[256,256]{1,0:T(8,128)} %get-tuple-element.75.v0_ref.v0, f32[256,256]{1,0:T(8,128)} %get-tuple-element.76.p_ref.p01), custom_call_target="tpu_custom_call" | custom-call | tf_op jit(solution)/shard_map/corner_d/pallas_call | solution.py:93
  171.1 2.2 table_sums.1
  173.2 1.3 collective-permute-start.29
  174.5 1.3 collective-permute-start.28
  175.8 1.3 collective-permute-start.27
  177.1 1.3 collective-permute-start.26
  178.4 1.3 collective-permute-start.25
  179.7 6.7 %factor.1 = f32[3,3,256,256]{3,2,1,0:T(8,128)} custom-call(s32[14]{0:T(128)} %concatenate.36.info, f32[3,3,256,256]{3,2,1,0:T(8,128)} %bitcast.67, f32[2,512,256]{2,1,0:T(8,128)} %get-tuple-element.86.xi, f32[2,512,256]{2,1,0:T(8,128)} %get-tuple-element.87.xj, f32[256,256]{1,0:T(8,128)} %get-tuple-element.75.v0_ref.v0, f32[256,256]{1,0:T(8,128)} %get-tuple-element.88.v1, ...), custom_call_target="tpu_custom_call" | custom-call | tf_op jit(solution)/shard_map/factor/pallas_call | solution.py:93
  186.5 4.9 %collective-permute-done.29.refs_7_ = f32[112,256]{1,0:T(8,128)S(1)} collective-permute-done((f32[112,256]{1,0:T(8,128)}, f32[112,256]{1,0:T(8,128)S(1)}, u32[]{:S(2)}, u32[]{:S(2)}) %collective-permute-start.29) | collective-permute-done | bytes 114720 | tf_op jit(solution)/shard_map/ppermute | solution.py:461
  191.4 1.3 collective-permute-start.24
  192.7 1.3 collective-permute-start.23
  194.1 4.3 %collective-permute-done.24.refs_2_ = f32[112,256]{1,0:T(8,128)S(1)} collective-permute-done((f32[112,256]{1,0:T(8,128)S(1)}, f32[112,256]{1,0:T(8,128)S(1)}, u32[]{:S(2)}, u32[]{:S(2)}) %collective-permute-start.24) | collective-permute-done | bytes 114720 | tf_op jit(solution)/shard_map/ppermute | solution.py:461
  198.4 3.3 %collective-permute-done.23.refs_1_ = f32[112,256]{1,0:T(8,128)S(1)} collective-permute-done((f32[112,256]{1,0:T(8,128)S(1)}, f32[112,256]{1,0:T(8,128)S(1)}, u32[]{:S(2)}, u32[]{:S(2)}) %collective-permute-start.23) | collective-permute-done | bytes 114720 | tf_op jit(solution)/shard_map/ppermute | solution.py:461
  202.3 2.6 %joined.1.mine = f32[1280,256]{1,0:T(8,128)} custom-call(f32[112,256]{1,0:T(8,128)} %get-tuple-element.93.refs_0_, f32[112,256]{1,0:T(8,128)} %copy-done.19, f32[112,256]{1,0:T(8,128)} %copy-done.18, f32[112,256]{1,0:T(8,128)} %copy-done.17, f32[112,256]{1,0:T(8,128)} %copy-done.16, f32[112,256]{1,0:T(8,128)} %copy-done.15, f32[112,256]{1,0:T(8,128)} %copy-done.14, ...), custom_call_target="tpu_custom_call" | custom-call | tf_op jit(solution)/shard_map/joined/pallas_call | solution.py:93
  205.4 2.9 %collective-permute-done.30.other = f32[1280,256]{1,0:T(8,128)S(1)} collective-permute-done((f32[1280,256]{1,0:T(8,128)}, f32[1280,256]{1,0:T(8,128)S(1)}, u32[]{:S(2)}, u32[]{:S(2)}) %collective-permute-start.30) | collective-permute-done | bytes 1310752 | tf_op jit(solution)/shard_map/ppermute | solution.py:382
  208.3 1.1 copy-done.6
  209.3 11.2 %grad.1 = f32[3,3,256,256]{3,2,1,0:T(8,128)} custom-call(s32[14]{0:T(128)} %concatenate.36.info, f32[3,3,256,256]{3,2,1,0:T(8,128)} %bitcast.62, f32[1280,256]{1,0:T(8,128)} %joined.1.mine, f32[1280,256]{1,0:T(8,128)} %copy-done.6, f32[512,256]{1,0:T(8,128)} %bitcast.65, f32[512,256]{1,0:T(8,128)} %copy-done.5, f32[256,256]{1,0:T(8,128)} %copy-done.7, ...), custom_call_target="tpu_custom_call" | custom-call | tf_op jit(solution)/shard_map/grad/pallas_call | solution.py:93
  (100 shorter events, 4.3 us)
Async XLA Ops:
  3.0 13.1 %collective-permute-start = (f32[96,256]{1,0:T(8,128)S(1)}, f32[96,256]{1,0:T(8,128)S(1)}, u32[]{:S(2)}, u32[]{:S(2)}) collective-permute-start(f32[96,256]{1,0:T(8,128)S(1)} %pad_maximum_fusion.1), channel_id=1, source_target_pairs={{0,2},{1,3},{16,18},{17,19},{32,34},{33,35},{48,50},{49,51},{64,66... | collective-permute-start | bytes 294920 | tf_op jit(solution)/shard_map/ppermute | solution.py:418
  7.4 10.0 %collective-permute-start.1 = (f32[96,256]{1,0:T(8,128)S(1)}, f32[96,256]{1,0:T(8,128)S(1)}, u32[]{:S(2)}, u32[]{:S(2)}) collective-permute-start(f32[96,256]{1,0:T(8,128)S(1)} %pad_maximum_fusion.2), channel_id=1, source_target_pairs={{0,4},{1,5},{16,20},{17,21},{32,36},{33,37},{48,52},{49,53},{64,68... | collective-permute-start | bytes 294920 | tf_op jit(solution)/shard_map/ppermute | solution.py:418
  9.4 9.3 %collective-permute-start.2 = (f32[96,256]{1,0:T(8,128)S(1)}, f32[96,256]{1,0:T(8,128)S(1)}, u32[]{:S(2)}, u32[]{:S(2)}) collective-permute-start(f32[96,256]{1,0:T(8,128)S(1)} %pad_maximum_fusion.3), channel_id=1, source_target_pairs={{0,6},{1,7},{16,22},{17,23},{32,38},{33,39},{48,54},{49,55},{64,70... | collective-permute-start | bytes 294920 | tf_op jit(solution)/shard_map/ppermute | solution.py:418
  11.5 7.2 %collective-permute-start.3 = (f32[96,256]{1,0:T(8,128)S(1)}, f32[96,256]{1,0:T(8,128)S(1)}, u32[]{:S(2)}, u32[]{:S(2)}) collective-permute-start(f32[96,256]{1,0:T(8,128)S(1)} %pad_maximum_fusion.4), channel_id=1, source_target_pairs={{0,8},{1,9},{16,24},{17,25},{32,40},{33,41},{48,56},{49,57},{64,72... | collective-permute-start | bytes 294920 | tf_op jit(solution)/shard_map/ppermute | solution.py:418
  14.7 4.0 %collective-permute-start.4 = (f32[96,256]{1,0:T(8,128)S(1)}, f32[96,256]{1,0:T(8,128)S(1)}, u32[]{:S(2)}, u32[]{:S(2)}) collective-permute-start(f32[96,256]{1,0:T(8,128)S(1)} %pad_maximum_fusion.5), channel_id=1, source_target_pairs={{0,10},{1,11},{16,26},{17,27},{32,42},{33,43},{48,58},{49,59},{64,... | collective-permute-start | bytes 294920 | tf_op jit(solution)/shard_map/ppermute | solution.py:418
  16.1 3.9 %collective-permute-start.5 = (f32[96,256]{1,0:T(8,128)S(1)}, f32[96,256]{1,0:T(8,128)S(1)}, u32[]{:S(2)}, u32[]{:S(2)}) collective-permute-start(f32[96,256]{1,0:T(8,128)S(1)} %pad_maximum_fusion.6), channel_id=1, source_target_pairs={{0,12},{1,13},{16,28},{17,29},{32,44},{33,45},{48,60},{49,61},{64,... | collective-permute-start | bytes 294920 | tf_op jit(solution)/shard_map/ppermute | solution.py:418
  17.4 4.7 %collective-permute-start.6 = (f32[96,256]{1,0:T(8,128)S(1)}, f32[96,256]{1,0:T(8,128)S(1)}, u32[]{:S(2)}, u32[]{:S(2)}) collective-permute-start(f32[96,256]{1,0:T(8,128)S(1)} %pad_maximum_fusion.7), channel_id=1, source_target_pairs={{0,14},{1,15},{16,30},{17,31},{32,46},{33,47},{48,62},{49,63},{64,... | collective-permute-start | bytes 294920 | tf_op jit(solution)/shard_map/ppermute | solution.py:418
  22.2 7.1 %collective-permute-start.7 = (f32[64,256]{1,0:T(8,128)S(1)}, f32[64,256]{1,0:T(8,128)S(1)}, u32[]{:S(2)}, u32[]{:S(2)}) collective-permute-start(f32[64,256]{1,0:T(8,128)S(1)} %slice.190), channel_id=1, source_target_pairs={{0,8},{1,9},{2,10},{3,11},{4,12},{5,13},{6,14},{7,15},{8,0},{9,1},... | collective-permute-start | bytes 196616 | tf_op jit(solution)/shard_map/ppermute | solution.py:382
  22.3 7.1 %collective-permute-start.8 = (f32[64,256]{1,0:T(8,128)S(1)}, f32[64,256]{1,0:T(8,128)S(1)}, u32[]{:S(2)}, u32[]{:S(2)}) collective-permute-start(f32[64,256]{1,0:T(8,128)S(1)} %slice.190), channel_id=1, source_target_pairs={{0,0},{1,16},{2,32},{3,48},{4,64},{5,80},{6,96},{7,112},{8,128},{9... | collective-permute-start | bytes 196616 | tf_op jit(solution)/shard_map/ppermute | solution.py:386
  30.7 35.6 %all-to-all-start = ((f32[16,96,256]{2,1,0:T(8,128)}), f32[16,96,256]{2,1,0:T(8,128)S(1)}, u32[]{:S(2)}, u32[]{:S(2)}) async-start(f32[16,96,256]{2,1,0:T(8,128)} %broadcast_in_dim.19), calls=%async_computation | async-start | bytes 3145728 | tf_op jit(solution)/shard_map/all_to_all | solution.py:425
  46.6 5.1 %collective-permute-start.9 = (f32[128,256]{1,0:T(8,128)S(1)}, f32[128,256]{1,0:T(8,128)S(1)}, u32[]{:S(2)}, u32[]{:S(2)}) collective-permute-start(f32[128,256]{1,0:T(8,128)S(1)} %pad_maximum_fusion), channel_id=1, source_target_pairs={{0,2},{1,3},{2,0},{3,1},{4,6},{5,7},{6,4},{7,5},{8,10},{9,11},{10,... | collective-permute-start | bytes 393224 | tf_op jit(solution)/shard_map/ppermute | solution.py:382
  46.8 26.7 %copy-start.3 = (f32[2,1,256,256]{3,2,1,0:T(8,128)}, f32[2,1,256,256]{3,2,1,0:T(8,128)S(1)}, u32[]{:S(2)}) copy-start(f32[2,1,256,256]{3,2,1,0:T(8,128)S(1)} %constant_dynamic-slice_fusion) | copy-start | bytes 1572868
  46.8 16.1 %collective-permute-start.11 = (f32[128,256]{1,0:T(8,128)S(1)}, f32[128,256]{1,0:T(8,128)S(1)}, u32[]{:S(2)}, u32[]{:S(2)}) collective-permute-start(f32[128,256]{1,0:T(8,128)S(1)} %pad_maximum_fusion), channel_id=1, source_target_pairs={{0,6},{1,7},{2,4},{3,5},{4,2},{5,3},{6,0},{7,1},{8,14},{9,15},{10,... | collective-permute-start | bytes 393224 | tf_op jit(solution)/shard_map/ppermute | solution.py:382
  50.8 11.4 %collective-permute-start.10 = (f32[128,256]{1,0:T(8,128)S(1)}, f32[128,256]{1,0:T(8,128)S(1)}, u32[]{:S(2)}, u32[]{:S(2)}) collective-permute-start(f32[128,256]{1,0:T(8,128)S(1)} %pad_maximum_fusion), channel_id=1, source_target_pairs={{0,4},{1,5},{2,6},{3,7},{4,0},{5,1},{6,2},{7,3},{8,12},{9,13},{10,... | collective-permute-start | bytes 393224 | tf_op jit(solution)/shard_map/ppermute | solution.py:382
  63.6 9.9 %collective-permute-start.12 = (f32[512,256]{1,0:T(8,128)}, f32[512,256]{1,0:T(8,128)}, u32[]{:S(2)}, u32[]{:S(2)}) collective-permute-start(f32[512,256]{1,0:T(8,128)} %constant_dynamic-update-slice_fusion.own), channel_id=1, source_target_pairs={{0,1},{1,0},{2,3},{3,2},{4,5},{5,4},{6,7},{7,6},{8,9},{9,8},{10,11... | collective-permute-start | bytes 1572872 | tf_op jit(solution)/shard_map/ppermute | solution.py:382
  65.2 8.2 %collective-permute-start.13 = (f32[512,256]{1,0:T(8,128)S(1)}, f32[512,256]{1,0:T(8,128)S(1)}, u32[]{:S(2)}, u32[]{:S(2)}) collective-permute-start(f32[512,256]{1,0:T(8,128)S(1)} %bitcast.63), channel_id=1, source_target_pairs={{0,1},{1,0},{2,3},{3,2},{4,5},{5,4},{6,7},{7,6},{8,9},{9,8},{10,11... | collective-permute-start | bytes 1572872 | tf_op jit(solution)/shard_map/ppermute | solution.py:382
  66.3 7.2 %copy-start = (f32[16,96,256]{2,1,0:T(8,128)}, f32[16,96,256]{2,1,0:T(8,128)S(1)}, u32[]{:S(2)}) copy-start(f32[16,96,256]{2,1,0:T(8,128)S(1)} %all-to-all-done.cols) | copy-start | bytes 4718596
  67.2 20.7 %all-to-all-start.2 = ((f32[8,64,256]{2,1,0:T(8,128)}), f32[8,64,256]{2,1,0:T(8,128)S(1)}, u32[]{:S(2)}, u32[]{:S(2)}) async-start(f32[8,64,256]{2,1,0:T(8,128)} %broadcast_in_dim.20), calls=%async_computation.2 | async-start | bytes 1048576 | tf_op jit(solution)/shard_map/all_to_all | solution.py:431
  73.5 0.8 copy-start.5
  82.8 10.7 %copy-start.8 = (f32[4,2,112,256]{3,2,1,0:T(8,128)S(1)}, f32[4,2,112,256]{3,2,1,0:T(8,128)}, u32[]{:S(2)}) copy-start(f32[4,2,112,256]{3,2,1,0:T(8,128)} %get-tuple-element.53) | copy-start | bytes 2752516
  82.8 10.7 %collective-permute-start.14 = (f32[4,2,112,256]{3,2,1,0:T(8,128)}, f32[4,2,112,256]{3,2,1,0:T(8,128)}, u32[]{:S(2)}, u32[]{:S(2)}) collective-permute-start(f32[4,2,112,256]{3,2,1,0:T(8,128)} %get-tuple-element.54), channel_id=1, source_target_pairs={{0,1},{1,0},{2,3},{3,2},{4,5},{5,4},{6,7},{7,6},{8,9},{9,8},{10,11... | collective-permute-start | bytes 2752520 | tf_op jit(solution)/shard_map/ppermute | solution.py:382
  87.9 7.8 %copy-start.4 = (f32[8,64,256]{2,1,0:T(8,128)}, f32[8,64,256]{2,1,0:T(8,128)S(1)}, u32[]{:S(2)}) copy-start(f32[8,64,256]{2,1,0:T(8,128)S(1)} %all-to-all-done.2.own) | copy-start | bytes 1572868
  87.9 32.3 %all-to-all-start.1 = ((f32[16,88,256]{2,1,0:T(8,128)}), f32[16,88,256]{2,1,0:T(8,128)S(1)}, u32[]{:S(2)}, u32[]{:S(2)}) async-start(f32[16,88,256]{2,1,0:T(8,128)} %get-tuple-element.52), calls=%async_computation.1 | async-start | bytes 2883584 | tf_op jit(solution)/shard_map/all_to_all | solution.py:435
  95.6 7.3 %collective-permute-start.18 = (f32[8,64,256]{2,1,0:T(8,128)S(1)}, f32[8,64,256]{2,1,0:T(8,128)S(1)}, u32[]{:S(2)}, u32[]{:S(2)}) collective-permute-start(f32[8,64,256]{2,1,0:T(8,128)S(1)} %all-to-all-done.2.own), channel_id=1, source_target_pairs={{0,1},{1,0},{2,3},{3,2},{4,5},{5,4},{6,7},{7,6},{8,9},{9,8},{10,11... | collective-permute-start | bytes 1572872 | tf_op jit(solution)/shard_map/ppermute | solution.py:382
  98.4 19.7 %collective-permute-start.15 = (f32[2,112,256]{2,1,0:T(8,128)}, f32[2,112,256]{2,1,0:T(8,128)S(1)}, u32[]{:S(2)}, u32[]{:S(2)}) collective-permute-start(f32[2,112,256]{2,1,0:T(8,128)} %get-tuple-element.56), channel_id=1, source_target_pairs={{0,2},{1,3},{2,0},{3,1},{4,6},{5,7},{6,4},{7,5},{8,10},{9,11},{10,... | collective-permute-start | bytes 688136 | tf_op jit(solution)/shard_map/ppermute | solution.py:382
  98.7 19.4 %collective-permute-start.16 = (f32[2,112,256]{2,1,0:T(8,128)}, f32[2,112,256]{2,1,0:T(8,128)}, u32[]{:S(2)}, u32[]{:S(2)}) collective-permute-start(f32[2,112,256]{2,1,0:T(8,128)} %get-tuple-element.57), channel_id=1, source_target_pairs={{0,4},{1,5},{2,6},{3,7},{4,0},{5,1},{6,2},{7,3},{8,12},{9,13},{10,... | collective-permute-start | bytes 688136 | tf_op jit(solution)/shard_map/ppermute | solution.py:382
  98.7 19.4 %collective-permute-start.17 = (f32[2,112,256]{2,1,0:T(8,128)S(1)}, f32[2,112,256]{2,1,0:T(8,128)}, u32[]{:S(2)}, u32[]{:S(2)}) collective-permute-start(f32[2,112,256]{2,1,0:T(8,128)S(1)} %get-tuple-element.58), channel_id=1, source_target_pairs={{0,6},{1,7},{2,4},{3,5},{4,2},{5,3},{6,0},{7,1},{8,14},{9,15},{10,... | collective-permute-start | bytes 688136 | tf_op jit(solution)/shard_map/ppermute | solution.py:382
  103.0 1.6 copy-start.9
  103.0 24.5 %collective-permute-start.20 = (f32[256,256]{1,0:T(8,128)S(1)}, f32[256,256]{1,0:T(8,128)S(1)}, u32[]{:S(2)}, u32[]{:S(2)}) collective-permute-start(f32[256,256]{1,0:T(8,128)S(1)} %slice_bitcast_fusion.1), channel_id=1, source_target_pairs={{16,0},{17,1},{18,2},{19,3},{20,4},{21,5},{22,6},{23,7},{24,8},{25... | collective-permute-start | bytes 786440 | tf_op jit(solution)/shard_map/ppermute | solution.py:443
  119.9 7.5 %collective-permute-start.19 = (f32[112,256]{1,0:T(8,128)S(1)}, f32[112,256]{1,0:T(8,128)S(1)}, u32[]{:S(2)}, u32[]{:S(2)}) collective-permute-start(f32[112,256]{1,0:T(8,128)S(1)} %get-tuple-element.125), channel_id=1, source_target_pairs={{0,8},{1,9},{2,10},{3,11},{4,12},{5,13},{6,14},{7,15},{8,0},{9,1},... | collective-permute-start | bytes 344072 | tf_op jit(solution)/shard_map/ppermute | solution.py:382
  120.2 7.3 %copy-start.1 = (f32[16,88,256]{2,1,0:T(8,128)}, f32[16,88,256]{2,1,0:T(8,128)S(1)}, u32[]{:S(2)}) copy-start(f32[16,88,256]{2,1,0:T(8,128)S(1)} %all-to-all-done.1.by_col) | copy-start | bytes 4325380
  127.4 0.7 copy-start.11
  130.7 10.1 %copy-start.21 = (f32[64,256]{1,0:T(8,128)S(1)}, f32[64,256]{1,0:T(8,128)}, u32[]{:S(2)}) copy-start(f32[64,256]{1,0:T(8,128)} %get-tuple-element.79) | copy-start | bytes 196612
  130.7 39.3 %all-to-all-start.3 = ((f32[16,72,256]{2,1,0:T(8,128)}), f32[16,72,256]{2,1,0:T(8,128)S(1)}, u32[]{:S(2)}, u32[]{:S(2)}) async-start(f32[16,72,256]{2,1,0:T(8,128)} %get-tuple-element.71), calls=%async_computation.3 | async-start | bytes 2359296 | tf_op jit(solution)/shard_map/all_to_all | solution.py:450
  138.1 48.3 %copy-start.7 = (f32[256,256]{1,0:T(8,128)}, f32[256,256]{1,0:T(8,128)S(1)}, u32[]{:S(2)}) copy-start(f32[256,256]{1,0:T(8,128)S(1)} %broadcast_select_fusion.ea) | copy-start | bytes 786436
  138.2 31.8 %collective-permute-start.21 = (f32[256,256]{1,0:T(8,128)S(1)}, f32[256,256]{1,0:T(8,128)S(1)}, u32[]{:S(2)}, u32[]{:S(2)}) collective-permute-start(f32[256,256]{1,0:T(8,128)S(1)} %broadcast_select_fusion.ea), channel_id=1, source_target_pairs={{0,1},{1,0},{2,3},{3,2},{4,5},{5,4},{6,7},{7,6},{8,9},{9,8},{10,11... | collective-permute-start | bytes 786440 | tf_op jit(solution)/shard_map/ppermute | solution.py:382
  140.8 29.1 %collective-permute-start.22 = (f32[64,256]{1,0:T(8,128)S(1)}, f32[64,256]{1,0:T(8,128)S(1)}, u32[]{:S(2)}, u32[]{:S(2)}) collective-permute-start(f32[64,256]{1,0:T(8,128)S(1)} %copy-done.21), channel_id=1, source_target_pairs={{0,0},{1,16},{2,32},{3,48},{4,64},{5,80},{6,96},{7,112},{8,128},{9... | collective-permute-start | bytes 196616 | tf_op jit(solution)/shard_map/ppermute | solution.py:386
  170.0 0.6 copy-start.20
  170.0 16.5 %copy-start.10 = (f32[256,256]{1,0:T(8,128)}, f32[256,256]{1,0:T(8,128)S(1)}, u32[]{:S(2)}) copy-start(f32[256,256]{1,0:T(8,128)S(1)} %collective-permute-done.21.eo) | copy-start | bytes 786436
  170.0 1.1 copy-start.2
  173.2 18.2 %collective-permute-start.29 = (f32[112,256]{1,0:T(8,128)}, f32[112,256]{1,0:T(8,128)S(1)}, u32[]{:S(2)}, u32[]{:S(2)}) collective-permute-start(f32[112,256]{1,0:T(8,128)} %get-tuple-element.93.refs_0_), channel_id=1, source_target_pairs={{14,0},{15,1},{30,16},{31,17},{46,32},{47,33},{62,48},{63,49},{78,... | collective-permute-start | bytes 344072 | tf_op jit(solution)/shard_map/ppermute | solution.py:461
  174.5 18.2 %collective-permute-start.28 = (f32[112,256]{1,0:T(8,128)}, f32[112,256]{1,0:T(8,128)S(1)}, u32[]{:S(2)}, u32[]{:S(2)}) collective-permute-start(f32[112,256]{1,0:T(8,128)} %get-tuple-element.93.refs_0_), channel_id=1, source_target_pairs={{12,0},{13,1},{28,16},{29,17},{44,32},{45,33},{60,48},{61,49},{76,... | collective-permute-start | bytes 344072 | tf_op jit(solution)/shard_map/ppermute | solution.py:461
  175.8 18.2 %collective-permute-start.27 = (f32[112,256]{1,0:T(8,128)}, f32[112,256]{1,0:T(8,128)S(1)}, u32[]{:S(2)}, u32[]{:S(2)}) collective-permute-start(f32[112,256]{1,0:T(8,128)} %get-tuple-element.93.refs_0_), channel_id=1, source_target_pairs={{10,0},{11,1},{26,16},{27,17},{42,32},{43,33},{58,48},{59,49},{74,... | collective-permute-start | bytes 344072 | tf_op jit(solution)/shard_map/ppermute | solution.py:461
  177.1 16.9 %collective-permute-start.26 = (f32[112,256]{1,0:T(8,128)}, f32[112,256]{1,0:T(8,128)S(1)}, u32[]{:S(2)}, u32[]{:S(2)}) collective-permute-start(f32[112,256]{1,0:T(8,128)} %get-tuple-element.93.refs_0_), channel_id=1, source_target_pairs={{8,0},{9,1},{24,16},{25,17},{40,32},{41,33},{56,48},{57,49},{72,64... | collective-permute-start | bytes 344072 | tf_op jit(solution)/shard_map/ppermute | solution.py:461
  178.4 15.6 %collective-permute-start.25 = (f32[112,256]{1,0:T(8,128)}, f32[112,256]{1,0:T(8,128)S(1)}, u32[]{:S(2)}, u32[]{:S(2)}) collective-permute-start(f32[112,256]{1,0:T(8,128)} %get-tuple-element.93.refs_0_), channel_id=1, source_target_pairs={{6,0},{7,1},{22,16},{23,17},{38,32},{39,33},{54,48},{55,49},{70,64... | collective-permute-start | bytes 344072 | tf_op jit(solution)/shard_map/ppermute | solution.py:461
  179.7 11.7 %copy-start.12 = (f32[112,256]{1,0:T(8,128)S(1)}, f32[112,256]{1,0:T(8,128)}, u32[]{:S(2)}) copy-start(f32[112,256]{1,0:T(8,128)} %get-tuple-element.93.refs_0_) | copy-start | bytes 344068
  191.4 10.3 %copy-start.13 = (f32[112,256]{1,0:T(8,128)}, f32[112,256]{1,0:T(8,128)S(1)}, u32[]{:S(2)}) copy-start(f32[112,256]{1,0:T(8,128)S(1)} %collective-permute-done.29.refs_7_) | copy-start | bytes 344068
  191.4 7.0 %collective-permute-start.24 = (f32[112,256]{1,0:T(8,128)S(1)}, f32[112,256]{1,0:T(8,128)S(1)}, u32[]{:S(2)}, u32[]{:S(2)}) collective-permute-start(f32[112,256]{1,0:T(8,128)S(1)} %copy-done.12), channel_id=1, source_target_pairs={{4,0},{5,1},{20,16},{21,17},{36,32},{37,33},{52,48},{53,49},{68,64... | collective-permute-start | bytes 344072 | tf_op jit(solution)/shard_map/ppermute | solution.py:461
  192.7 9.0 %copy-start.14 = (f32[112,256]{1,0:T(8,128)}, f32[112,256]{1,0:T(8,128)S(1)}, u32[]{:S(2)}) copy-start(f32[112,256]{1,0:T(8,128)S(1)} %collective-permute-done.28.refs_6_) | copy-start | bytes 344068
  192.7 9.0 %collective-permute-start.23 = (f32[112,256]{1,0:T(8,128)S(1)}, f32[112,256]{1,0:T(8,128)S(1)}, u32[]{:S(2)}, u32[]{:S(2)}) collective-permute-start(f32[112,256]{1,0:T(8,128)S(1)} %copy-done.12), channel_id=1, source_target_pairs={{2,0},{3,1},{18,16},{19,17},{34,32},{35,33},{50,48},{51,49},{66,64... | collective-permute-start | bytes 344072 | tf_op jit(solution)/shard_map/ppermute | solution.py:461
  194.0 7.7 %copy-start.15 = (f32[112,256]{1,0:T(8,128)}, f32[112,256]{1,0:T(8,128)S(1)}, u32[]{:S(2)}) copy-start(f32[112,256]{1,0:T(8,128)S(1)} %collective-permute-done.27.refs_5_) | copy-start | bytes 344068
  194.0 7.7 %copy-start.16 = (f32[112,256]{1,0:T(8,128)}, f32[112,256]{1,0:T(8,128)S(1)}, u32[]{:S(2)}) copy-start(f32[112,256]{1,0:T(8,128)S(1)} %collective-permute-done.26.refs_4_) | copy-start | bytes 344068
  194.0 7.7 %copy-start.17 = (f32[112,256]{1,0:T(8,128)}, f32[112,256]{1,0:T(8,128)S(1)}, u32[]{:S(2)}) copy-start(f32[112,256]{1,0:T(8,128)S(1)} %collective-permute-done.25.refs_3_) | copy-start | bytes 344068
  198.4 3.4 %copy-start.18 = (f32[112,256]{1,0:T(8,128)}, f32[112,256]{1,0:T(8,128)S(1)}, u32[]{:S(2)}) copy-start(f32[112,256]{1,0:T(8,128)S(1)} %collective-permute-done.24.refs_2_) | copy-start | bytes 344068
  201.7 0.6 copy-start.19
  204.9 3.4 %collective-permute-start.30 = (f32[1280,256]{1,0:T(8,128)}, f32[1280,256]{1,0:T(8,128)S(1)}, u32[]{:S(2)}, u32[]{:S(2)}) collective-permute-start(f32[1280,256]{1,0:T(8,128)} %joined.1.mine), channel_id=1, source_target_pairs={{0,1},{1,0},{2,3},{3,2},{4,5},{5,4},{6,7},{7,6},{8,9},{9,8},{10,11... | collective-permute-start | bytes 3932168 | tf_op jit(solution)/shard_map/ppermute | solution.py:382
  208.3 1.1 copy-start.6
where the time goes:
time: 225 us; the launch traced here: 221 us
  starting transfers between devices  97.6 us (43%)
  Pallas kernels  62 us (28%)
  waiting for transfers between devices  39.9 us (18%)
  local copies, waits for them, and re-layouts  13.1 us (6%)
  other arithmetic  6.6 us (3%)
    pallas_call x9, Pallas kernels, run(): pl.pallas_call(body, grid=(1,), out_shape=outputs, in_specs=[SMEM if x.dt...  62 us
    ppermute x14, waiting for transfers between devices, flip(): return lax.ppermute(x, axis, [(i, i ^ m) for i in range(N)])  21.8 us
    ppermute x2, starting transfers between devices, transposed(): lax.ppermute(x, ('row', 'col'), [(r * N + c, c * N + r) for r in range(N)...  19.6 us
    ppermute x14, starting transfers between devices, flip(): return lax.ppermute(x, axis, [(i, i ^ m) for i in range(N)])  18.9 us
    ppermute x7, starting transfers between devices, on_device(): lax.ppermute(pieces[q], 'col', [(a, 2 * q + a) for a in range(2)])  15.5 us
    all_to_all x1, starting transfers between devices, on_device(): cols = lax.all_to_all(jnp.broadcast_to(col_send, (N, 96, B)), 'row', 0, 0)  14.7 us
    ppermute x7, waiting for transfers between devices, to_owner(): return lax.ppermute(x, 'col', [(2 * q + a, a) for a in range(2)])  12.6 us
    ppermute x7, starting transfers between devices, to_owner(): return lax.ppermute(x, 'col', [(2 * q + a, a) for a in range(2)])  9.02 us
  transfers between devices with their start and end apart: 35, of which 11 were waited for; matrix products, arithmetic and copies ran while one was open for 5% of the time, Pallas kernels for 20%

commit v1 on v0

--- a/solution.py
+++ b/solution.py
@@ -89,7 +89,7 @@
     return pl.BlockSpec(x.shape, lambda i: (0,) * len(x.shape), pipeline_mode=pl.Buffered(1))
 
 
-def run(body, name, outputs, scratch, *args):
+def run(body, name, outputs, scratch, *args, grant=16):
     return pl.pallas_call(
         body,
         grid=(1,),
@@ -97,7 +97,7 @@
         in_specs=[SMEM if x.dtype == jnp.int32 else whole(x) for x in args],
         out_specs=jax.tree.map(whole, outputs),
         scratch_shapes=scratch,
-        compiler_params=PARAMS,
+        compiler_params=pltpu.CompilerParams(vmem_limit_bytes=grant * 1024 * 1024),
         name=name,
     )(*args)
 
@@ -220,7 +220,7 @@
 
 def partials(*args):
     outputs = [array(2, 512, B)] * 2 + [array(4, 2, 112, B)] * 2 + [array(16, 88, B)]
-    return run(partial_kernel, "partials", outputs, [pltpu.VMEM((2, 4, 2, 112, B), f32)], *args)
+    return run(partial_kernel, "partials", outputs, [pltpu.VMEM((2, 4, 2, 112, B), f32)], *args, grant=60)
 
 
 def sums_kernel(by_col, near, came, h_row, h_col, td):
@@ -305,7 +305,7 @@
 
 
 def factor_of(*args):
-    return run(factor_kernel, "factor", array(3, 3, B, B), [], *args)
+    return run(factor_kernel, "factor", array(3, 3, B, B), [], *args, grant=60)
 
 
 def pull_cholesky(l, v, bar):
@@ -317,7 +317,7 @@
     return 0.5 * (full + full.T)
 
 
-def grad_kernel(info, cot, mine, other, ca, co, ea, eo, v0, v1, u, p01, l0, l1, out):
+def grad_kernel(info, cot, mine, other, d_own, d_far, ca, co, ea, eo, v0, v1, u, p01, l0, l1, out):
     row, col = info[0], info[1]
     sr = info[2]
     for i in range(3):
@@ -348,7 +348,8 @@
         @pl.when(row < 2)
         def _():
             t = jnp.concatenate([x[112 * q + 64 : 112 * q + 112] for x in (left, right) for q in range(8)], 0)
-            d = jnp.concatenate([left[896:], right[896:]], 0)
+            d0, d1 = d_own[...], d_far[...]
+            d = jnp.concatenate([jnp.where(first, d0, d1), jnp.where(first, d1, d0)], 0)
             t00, t01, t11 = t[:B], t[B : 2 * B], t[2 * B :]
             d00, d10, d11 = d[:B], d[B : 2 * B], d[2 * B :]
             c10 = jnp.where(first, ea[...], eo[...])
@@ -372,7 +373,7 @@
 
 
 def grad_of(*args):
-    return run(grad_kernel, "grad", array(3, 3, B, B), [], *args)
+    return run(grad_kernel, "grad", array(3, 3, B, B), [], *args, grant=60)
 
 
 Z_GROUPS = [list(range(0, N, 2)), list(range(1, N, 2))]
@@ -452,6 +453,7 @@
     ea = jnp.where(row == 0, from_one, edge)
     eo = flip(ea, "col", 1)
     a1, v1 = corner_call(corner_c_kernel, "corner_c", 2, 0, x1)
+    h_col, a1 = lax.optimization_barrier((h_col, a1))
     v1, l1, u = corner_call(corner_d_kernel, "corner_d", 3, 1, a1, v1, v0, p01)
     td, u, eo, h_col = lax.optimization_barrier((td, u, eo, h_col))
 
@@ -461,12 +463,13 @@
         return lax.ppermute(x, "col", [(2 * q + a, a) for a in range(2)])
 
     pieces = [to_owner(send, q) for q in range(3, 8)]
+    d_far = flip(d_half, "col", 1)
     factor_out = factor_of(info, kernel3, xi, xj, v0, v1, u, p01, l0, l1)
     again, factor_out = lax.optimization_barrier((send, factor_out))
     pieces = [send] + [to_owner(again, q) for q in range(1, 3)] + pieces
-    mine = joined(pieces + [d_half])
+    mine = joined(pieces)
     theirs = flip(mine, "col", 1)
-    grad_out = grad_of(info, cot3, mine, theirs, ca, co, ea, eo, v0, v1, u, p01, l0, l1)
+    grad_out = grad_of(info, cot3, mine, theirs, d_half, d_far, ca, co, ea, eo, v0, v1, u, p01, l0, l1)
     return (factor_out.reshape(kernel.shape), grad_out.reshape(kernel.shape))
 
 

time: 225 us -> 211 us (0.938)
  Pallas kernels: 62 us -> 50.9 us
    pallas_call x9, Pallas kernels: 62 us -> 50.9 us  [run(): pl.pallas_call(body, grid=(1,), out_shape=outputs, in_specs=[SMEM if x.dt...]
    ppermute x14 -> x15, waiting for transfers between devices: 21.8 us -> 21.5 us  [flip(): return lax.ppermute(x, axis, [(i, i ^ m) for i in range(N)])]
    unnamed x47 -> x33, local copies, waits for them, and re-layouts: 6.21 us -> 6.49 us
    ppermute x14 -> x15, starting transfers between devices: 18.9 us -> 19.1 us  [flip(): return lax.ppermute(x, axis, [(i, i ^ m) for i in range(N)])]
  transfers between devices with their start and end apart: 35 -> 36, of which waited for: 11 -> 11; matrix products, arithmetic and copies ran while one was open for 5% -> 5% of each run, Pallas kernels for 20% -> 18%
where the time goes in v1:
time: 211 us; the launch traced here: 208 us
  starting transfers between devices  98.6 us (47%)
  Pallas kernels  50.9 us (24%)
  waiting for transfers between devices  39.4 us (19%)
  local copies, waits for them, and re-layouts  12.6 us (6%)
  other arithmetic  5.14 us (2%)
    pallas_call x9, Pallas kernels, run(): pl.pallas_call(body, grid=(1,), out_shape=outputs, in_specs=[SMEM if x.dt...  50.9 us
    ppermute x15, waiting for transfers between devices, flip(): return lax.ppermute(x, axis, [(i, i ^ m) for i in range(N)])  21.5 us
    ppermute x2, starting transfers between devices, transposed(): lax.ppermute(x, ('row', 'col'), [(r * N + c, c * N + r) for r in range(N)...  19.8 us
    ppermute x15, starting transfers between devices, flip(): return lax.ppermute(x, axis, [(i, i ^ m) for i in range(N)])  19.1 us
    ppermute x7, starting transfers between devices, on_device(): lax.ppermute(pieces[q], 'col', [(a, 2 * q + a) for a in range(2)])  15.5 us
    all_to_all x1, starting transfers between devices, on_device(): cols = lax.all_to_all(jnp.broadcast_to(col_send, (N, 96, B)), 'row', 0, 0)  14.7 us
    ppermute x7, waiting for transfers between devices, to_owner(): return lax.ppermute(x, 'col', [(2 * q + a, a) for a in range(2)])  12.4 us
    ppermute x7, starting transfers between devices, to_owner(): return lax.ppermute(x, 'col', [(2 * q + a, a) for a in range(2)])  9.03 us
  transfers between devices with their start and end apart: 36, of which 11 were waited for; matrix products, arithmetic and copies ran while one was open for 5% of the time, Pallas kernels for 18%

profile of v1, /device:TPU:1, one launch (start us, length us, event | category | flops | bytes accessed | tf_op | source)
XLA Modules:
  0.0 208.2 jit_solution(15466162696112216178)
XLA Ops:
  0.7 0.7 fusion.16
  1.6 1.3 fusion
  3.0 4.4 %collective-permute-start = (f32[96,256]{1,0:T(8,128)S(1)}, f32[96,256]{1,0:T(8,128)S(1)}, u32[]{:S(2)}, u32[]{:S(2)}) collective-permute-start(f32[96,256]{1,0:T(8,128)S(1)} %pad_maximum_fusion.1), channel_id=1, source_target_pairs={{0,2},{1,3},{16,18},{17,19},{32,34},{33,35},{48,50},{49,51},{64,66... | collective-permute-start | bytes 294920 | tf_op jit(solution)/shard_map/ppermute | solution.py:419
  7.4 2.0 collective-permute-start.1
  9.4 2.0 collective-permute-start.2
  11.5 3.2 %collective-permute-start.3 = (f32[96,256]{1,0:T(8,128)S(1)}, f32[96,256]{1,0:T(8,128)S(1)}, u32[]{:S(2)}, u32[]{:S(2)}) collective-permute-start(f32[96,256]{1,0:T(8,128)S(1)} %pad_maximum_fusion.4), channel_id=1, source_target_pairs={{0,8},{1,9},{16,24},{17,25},{32,40},{33,41},{48,56},{49,57},{64,72... | collective-permute-start | bytes 294920 | tf_op jit(solution)/shard_map/ppermute | solution.py:419
  14.7 1.3 collective-permute-start.4
  16.1 1.3 collective-permute-start.5
  17.4 1.3 collective-permute-start.6
  18.7 1.2 collective-permute-done.5
  20.0 2.1 %collective-permute-done.6 = f32[96,256]{1,0:T(8,128)S(1)} collective-permute-done((f32[96,256]{1,0:T(8,128)S(1)}, f32[96,256]{1,0:T(8,128)S(1)}, u32[]{:S(2)}, u32[]{:S(2)}) %collective-permute-start.6) | collective-permute-done | bytes 98336 | tf_op jit(solution)/shard_map/ppermute | solution.py:419
  22.3 5.2 %collective-permute-start.8 = (f32[64,256]{1,0:T(8,128)S(1)}, f32[64,256]{1,0:T(8,128)S(1)}, u32[]{:S(2)}, u32[]{:S(2)}) collective-permute-start(f32[64,256]{1,0:T(8,128)S(1)} %slice.190), channel_id=1, source_target_pairs={{0,0},{1,16},{2,32},{3,48},{4,64},{5,80},{6,96},{7,112},{8,128},{9... | collective-permute-start | bytes 196616 | tf_op jit(solution)/shard_map/ppermute | solution.py:387
  27.4 1.8 collective-permute-done.7
  29.4 1.3 broadcast_in_dim.19
  30.7 14.7 %all-to-all-start = ((f32[16,96,256]{2,1,0:T(8,128)}), f32[16,96,256]{2,1,0:T(8,128)S(1)}, u32[]{:S(2)}, u32[]{:S(2)}) async-start(f32[16,96,256]{2,1,0:T(8,128)} %broadcast_in_dim.19), calls=%async_computation | async-start | bytes 3145728 | tf_op jit(solution)/shard_map/all_to_all | solution.py:426
  45.4 1.2 slice.192
  46.8 4.0 %collective-permute-start.11 = (f32[128,256]{1,0:T(8,128)S(1)}, f32[128,256]{1,0:T(8,128)S(1)}, u32[]{:S(2)}, u32[]{:S(2)}) collective-permute-start(f32[128,256]{1,0:T(8,128)S(1)} %pad_maximum_fusion), channel_id=1, source_target_pairs={{0,6},{1,7},{2,4},{3,5},{4,2},{5,3},{6,0},{7,1},{8,14},{9,15},{10,... | collective-permute-start | bytes 393224 | tf_op jit(solution)/shard_map/ppermute | solution.py:383
  51.1 0.7 constant_dynamic-update-slice_fusion.3
  51.8 0.7 constant_dynamic-update-slice_fusion.2
  52.4 9.8 %collective-permute-done.10 = f32[128,256]{1,0:T(8,128)S(1)} collective-permute-done((f32[128,256]{1,0:T(8,128)S(1)}, f32[128,256]{1,0:T(8,128)S(1)}, u32[]{:S(2)}, u32[]{:S(2)}) %collective-permute-start.10) | collective-permute-done | bytes 131104 | tf_op jit(solution)/shard_map/ppermute | solution.py:383
  62.2 0.7 constant_dynamic-update-slice_fusion.1
  62.9 0.7 constant_dynamic-update-slice_fusion.own
  63.6 1.7 collective-permute-start.12
  65.6 0.6 concatenate.36.info
  66.2 0.9 broadcast_in_dim.20
  67.1 6.3 %all-to-all-start.2 = ((f32[8,64,256]{2,1,0:T(8,128)}), f32[8,64,256]{2,1,0:T(8,128)S(1)}, u32[]{:S(2)}, u32[]{:S(2)}) async-start(f32[8,64,256]{2,1,0:T(8,128)} %broadcast_in_dim.20), calls=%async_computation.2 | async-start | bytes 1048576 | tf_op jit(solution)/shard_map/all_to_all | solution.py:432
  73.5 0.8 copy-done.11
  74.3 8.5 %partials.1 = (f32[2,512,256]{2,1,0:T(8,128)}, f32[2,512,256]{2,1,0:T(8,128)}, f32[4,2,112,256]{3,2,1,0:T(8,128)}, f32[4,2,112,256]{3,2,1,0:T(8,128)}, f32[16,88,256]{2,1,0:T(8,128)}) custom-call(s32[14]{0:T(128)} %concatenate.36.info, f32[3,3,256,256]{3,2,1,0:T(8,128)} %bitcast.59, f32[512,256]{1,0:T(8,128)} %constant_dynamic-update-slice_fusion.own, ...), custom_call_target="tpu_custom_call" | custom-call | tf_op jit(solution)/shard_map/partials/pallas_call | solution.py:93
  82.8 3.0 %collective-permute-start.14 = (f32[4,2,112,256]{3,2,1,0:T(8,128)}, f32[4,2,112,256]{3,2,1,0:T(8,128)}, u32[]{:S(2)}, u32[]{:S(2)}) collective-permute-start(f32[4,2,112,256]{3,2,1,0:T(8,128)} %get-tuple-element.56), channel_id=1, source_target_pairs={{0,1},{1,0},{2,3},{3,2},{4,5},{5,4},{6,7},{7,6},{8,9},{9,8},{10,11... | collective-permute-start | bytes 2752520 | tf_op jit(solution)/shard_map/ppermute | solution.py:383
  85.8 2.1 %all-to-all-done.2.own = f32[8,64,256]{2,1,0:T(8,128)S(1)} async-done(((f32[8,64,256]{2,1,0:T(8,128)}), f32[8,64,256]{2,1,0:T(8,128)S(1)}, u32[]{:S(2)}, u32[]{:S(2)}) %all-to-all-start.2) | async-done | bytes 524320 | tf_op jit(solution)/shard_map/all_to_all | solution.py:432
  87.9 5.5 %all-to-all-start.1 = ((f32[16,88,256]{2,1,0:T(8,128)}), f32[16,88,256]{2,1,0:T(8,128)S(1)}, u32[]{:S(2)}, u32[]{:S(2)}) async-start(f32[16,88,256]{2,1,0:T(8,128)} %get-tuple-element.54), calls=%async_computation.1 | async-start | bytes 2883584 | tf_op jit(solution)/shard_map/all_to_all | solution.py:436
  93.4 1.7 fusion.1
  95.1 2.9 %collective-permute-start.18 = (f32[8,64,256]{2,1,0:T(8,128)S(1)}, f32[8,64,256]{2,1,0:T(8,128)S(1)}, u32[]{:S(2)}, u32[]{:S(2)}) collective-permute-start(f32[8,64,256]{2,1,0:T(8,128)S(1)} %all-to-all-done.2.own), channel_id=1, source_target_pairs={{0,1},{1,0},{2,3},{3,2},{4,5},{5,4},{6,7},{7,6},{8,9},{9,8},{10,11... | collective-permute-start | bytes 1572872 | tf_op jit(solution)/shard_map/ppermute | solution.py:383
  98.2 3.3 %collective-permute-start.17 = (f32[2,112,256]{2,1,0:T(8,128)S(1)}, f32[2,112,256]{2,1,0:T(8,128)S(1)}, u32[]{:S(2)}, u32[]{:S(2)}) collective-permute-start(f32[2,112,256]{2,1,0:T(8,128)S(1)} %get-tuple-element.60), channel_id=1, source_target_pairs={{0,6},{1,7},{2,4},{3,5},{4,2},{5,3},{6,0},{7,1},{8,14},{9,15},{10,... | collective-permute-start | bytes 688136 | tf_op jit(solution)/shard_map/ppermute | solution.py:383
  101.5 1.0 slice_bitcast_fusion.1
  102.5 1.5 collective-permute-start.20
  104.0 12.1 %corner_a.1 = (f32[256,256]{1,0:T(8,128)S(1)}, f32[256,256]{1,0:T(8,128)S(1)}, f32[256,256]{1,0:T(8,128)S(1)}, f32[256,256]{1,0:T(8,128)S(1)}) custom-call(s32[14]{0:T(128)S(1)} %copy-done.8, f32[8,64,256]{2,1,0:T(8,128)S(1)} %all-to-all-done.2.own, f32[8,64,256]{2,1,0:T(8,128)S(1)} %collective-permute-done.18.far), custom_call_target="tpu_custom_call" | custom-call | tf_op jit(solution)/shard_map/corner_a/pallas_call | solution.py:93
  116.3 0.6 copy-done.3
  117.1 7.3 %collective-permute-done.19.came = f32[112,256]{1,0:T(8,128)S(1)} collective-permute-done((f32[112,256]{1,0:T(8,128)S(1)}, f32[112,256]{1,0:T(8,128)S(1)}, u32[]{:S(2)}, u32[]{:S(2)}) %collective-permute-start.19) | collective-permute-done | bytes 114720 | tf_op jit(solution)/shard_map/ppermute | solution.py:383
  124.4 1.1 sums.1
  125.5 7.0 %all-to-all-start.3 = ((f32[16,72,256]{2,1,0:T(8,128)}), f32[16,72,256]{2,1,0:T(8,128)S(1)}, u32[]{:S(2)}, u32[]{:S(2)}) async-start(f32[16,72,256]{2,1,0:T(8,128)} %get-tuple-element.73), calls=%async_computation.3 | async-start | bytes 2359296 | tf_op jit(solution)/shard_map/all_to_all | solution.py:451
  132.5 1.1 broadcast_select_fusion.ea
  133.6 2.6 %collective-permute-start.22 = (f32[256,256]{1,0:T(8,128)S(1)}, f32[256,256]{1,0:T(8,128)}, u32[]{:S(2)}, u32[]{:S(2)}) collective-permute-start(f32[256,256]{1,0:T(8,128)S(1)} %broadcast_select_fusion.ea), channel_id=1, source_target_pairs={{0,1},{1,0},{2,3},{3,2},{4,5},{5,4},{6,7},{7,6},{8,9},{9,8},{10,11... | collective-permute-start | bytes 786440 | tf_op jit(solution)/shard_map/ppermute | solution.py:383
  136.2 14.6 %collective-permute-start.21 = (f32[64,256]{1,0:T(8,128)S(1)}, f32[64,256]{1,0:T(8,128)S(1)}, u32[]{:S(2)}, u32[]{:S(2)}) collective-permute-start(f32[64,256]{1,0:T(8,128)S(1)} %get-tuple-element.74), channel_id=1, source_target_pairs={{0,0},{1,16},{2,32},{3,48},{4,64},{5,80},{6,96},{7,112},{8,128},{9... | collective-permute-start | bytes 196616 | tf_op jit(solution)/shard_map/ppermute | solution.py:387
  150.8 5.5 %corner_c.1 = (f32[256,256]{1,0:T(8,128)S(1)}, f32[256,256]{1,0:T(8,128)S(1)}) custom-call(f32[256,256]{1,0:T(8,128)S(1)} %get-tuple-element.75.x_ref), custom_call_target="tpu_custom_call" | custom-call | tf_op jit(solution)/shard_map/corner_c/pallas_call | solution.py:93
  156.4 5.6 %corner_d.1 = (f32[256,256]{1,0:T(8,128)S(1)}, f32[256,256]{1,0:T(8,128)S(1)}, f32[256,256]{1,0:T(8,128)S(1)}) custom-call(f32[256,256]{1,0:T(8,128)S(1)} %get-tuple-element.77.a_in, f32[256,256]{1,0:T(8,128)S(1)} %get-tuple-element.78.v_in, f32[256,256]{1,0:T(8,128)S(1)} %get-tuple-element.79.v0_ref.v0, f32[256,256]{1,0:T(8,128)S(1)} %get-tuple-element.80.p_ref.p01), custom_call_target="tpu_custom_call" | custom-call | tf_op jit(solution)/shard_map/corner_d/pallas_call | solution.py:93
  162.0 0.7 copy-done.4
  162.8 0.7 copy-done.5
  163.5 1.3 collective-permute-start.29
  164.8 1.3 collective-permute-start.28
  166.1 1.3 collective-permute-start.27
  167.4 1.3 collective-permute-start.26
  168.7 1.3 collective-permute-start.25
  170.1 6.7 %factor.1 = f32[3,3,256,256]{3,2,1,0:T(8,128)} custom-call(s32[14]{0:T(128)} %concatenate.36.info, f32[3,3,256,256]{3,2,1,0:T(8,128)} %bitcast.67, f32[2,512,256]{2,1,0:T(8,128)} %get-tuple-element.90.xi, f32[2,512,256]{2,1,0:T(8,128)} %get-tuple-element.91.xj, f32[256,256]{1,0:T(8,128)} %copy-done.1, f32[256,256]{1,0:T(8,128)} %copy-done.4, ...), custom_call_target="tpu_custom_call" | custom-call | tf_op jit(solution)/shard_map/factor/pallas_call | solution.py:93
  176.8 4.7 %collective-permute-done.29.refs_7_ = f32[112,256]{1,0:T(8,128)S(1)} collective-permute-done((f32[112,256]{1,0:T(8,128)S(1)}, f32[112,256]{1,0:T(8,128)S(1)}, u32[]{:S(2)}, u32[]{:S(2)}) %collective-permute-start.29) | collective-permute-done | bytes 114720 | tf_op jit(solution)/shard_map/ppermute | solution.py:463
  181.5 1.3 collective-permute-start.24
  182.8 1.3 collective-permute-start.23
  184.1 4.3 %collective-permute-done.24.refs_2_ = f32[112,256]{1,0:T(8,128)S(1)} collective-permute-done((f32[112,256]{1,0:T(8,128)S(1)}, f32[112,256]{1,0:T(8,128)S(1)}, u32[]{:S(2)}, u32[]{:S(2)}) %collective-permute-start.24) | collective-permute-done | bytes 114720 | tf_op jit(solution)/shard_map/ppermute | solution.py:463
  188.4 3.4 %collective-permute-done.23.refs_1_ = f32[112,256]{1,0:T(8,128)S(1)} collective-permute-done((f32[112,256]{1,0:T(8,128)S(1)}, f32[112,256]{1,0:T(8,128)S(1)}, u32[]{:S(2)}, u32[]{:S(2)}) %collective-permute-start.23) | collective-permute-done | bytes 114720 | tf_op jit(solution)/shard_map/ppermute | solution.py:463
  191.9 0.6 collective-permute-start.30
  192.6 2.6 %collective-permute-done.31.d_far = f32[384,256]{1,0:T(8,128)S(1)} collective-permute-done((f32[384,256]{1,0:T(8,128)S(1)}, f32[384,256]{1,0:T(8,128)S(1)}, u32[]{:S(2)}, u32[]{:S(2)}) %collective-permute-start.31) | collective-permute-done | bytes 393248 | tf_op jit(solution)/shard_map/ppermute | solution.py:383
  195.1 0.8 copy-done.14
  195.9 0.9 copy-done.13
  196.8 11.2 %grad.1 = f32[3,3,256,256]{3,2,1,0:T(8,128)} custom-call(s32[14]{0:T(128)} %concatenate.36.info, f32[3,3,256,256]{3,2,1,0:T(8,128)} %bitcast.62, f32[896,256]{1,0:T(8,128)} %copy-done, f32[896,256]{1,0:T(8,128)} %copy-done.13, f32[384,256]{1,0:T(8,128)} %copy-done.7, f32[384,256]{1,0:T(8,128)} %copy-done.14, f32[512,256]{1,0:T(8,128)} %bitcast.65, ...), custom_call_target="tpu_custom_call" | custom-call | tf_op jit(solution)/shard_map/grad/pallas_call | solution.py:93
  (88 shorter events, 2.4 us)
Async XLA Ops:
  3.0 13.1 %collective-permute-start = (f32[96,256]{1,0:T(8,128)S(1)}, f32[96,256]{1,0:T(8,128)S(1)}, u32[]{:S(2)}, u32[]{:S(2)}) collective-permute-start(f32[96,256]{1,0:T(8,128)S(1)} %pad_maximum_fusion.1), channel_id=1, source_target_pairs={{0,2},{1,3},{16,18},{17,19},{32,34},{33,35},{48,50},{49,51},{64,66... | collective-permute-start | bytes 294920 | tf_op jit(solution)/shard_map/ppermute | solution.py:419
  7.4 10.0 %collective-permute-start.1 = (f32[96,256]{1,0:T(8,128)S(1)}, f32[96,256]{1,0:T(8,128)S(1)}, u32[]{:S(2)}, u32[]{:S(2)}) collective-permute-start(f32[96,256]{1,0:T(8,128)S(1)} %pad_maximum_fusion.2), channel_id=1, source_target_pairs={{0,4},{1,5},{16,20},{17,21},{32,36},{33,37},{48,52},{49,53},{64,68... | collective-permute-start | bytes 294920 | tf_op jit(solution)/shard_map/ppermute | solution.py:419
  9.4 9.3 %collective-permute-start.2 = (f32[96,256]{1,0:T(8,128)S(1)}, f32[96,256]{1,0:T(8,128)S(1)}, u32[]{:S(2)}, u32[]{:S(2)}) collective-permute-start(f32[96,256]{1,0:T(8,128)S(1)} %pad_maximum_fusion.3), channel_id=1, source_target_pairs={{0,6},{1,7},{16,22},{17,23},{32,38},{33,39},{48,54},{49,55},{64,70... | collective-permute-start | bytes 294920 | tf_op jit(solution)/shard_map/ppermute | solution.py:419
  11.5 7.2 %collective-permute-start.3 = (f32[96,256]{1,0:T(8,128)S(1)}, f32[96,256]{1,0:T(8,128)S(1)}, u32[]{:S(2)}, u32[]{:S(2)}) collective-permute-start(f32[96,256]{1,0:T(8,128)S(1)} %pad_maximum_fusion.4), channel_id=1, source_target_pairs={{0,8},{1,9},{16,24},{17,25},{32,40},{33,41},{48,56},{49,57},{64,72... | collective-permute-start | bytes 294920 | tf_op jit(solution)/shard_map/ppermute | solution.py:419
  14.7 4.0 %collective-permute-start.4 = (f32[96,256]{1,0:T(8,128)S(1)}, f32[96,256]{1,0:T(8,128)S(1)}, u32[]{:S(2)}, u32[]{:S(2)}) collective-permute-start(f32[96,256]{1,0:T(8,128)S(1)} %pad_maximum_fusion.5), channel_id=1, source_target_pairs={{0,10},{1,11},{16,26},{17,27},{32,42},{33,43},{48,58},{49,59},{64,... | collective-permute-start | bytes 294920 | tf_op jit(solution)/shard_map/ppermute | solution.py:419
  16.1 3.9 %collective-permute-start.5 = (f32[96,256]{1,0:T(8,128)S(1)}, f32[96,256]{1,0:T(8,128)S(1)}, u32[]{:S(2)}, u32[]{:S(2)}) collective-permute-start(f32[96,256]{1,0:T(8,128)S(1)} %pad_maximum_fusion.6), channel_id=1, source_target_pairs={{0,12},{1,13},{16,28},{17,29},{32,44},{33,45},{48,60},{49,61},{64,... | collective-permute-start | bytes 294920 | tf_op jit(solution)/shard_map/ppermute | solution.py:419
  17.4 4.7 %collective-permute-start.6 = (f32[96,256]{1,0:T(8,128)S(1)}, f32[96,256]{1,0:T(8,128)S(1)}, u32[]{:S(2)}, u32[]{:S(2)}) collective-permute-start(f32[96,256]{1,0:T(8,128)S(1)} %pad_maximum_fusion.7), channel_id=1, source_target_pairs={{0,14},{1,15},{16,30},{17,31},{32,46},{33,47},{48,62},{49,63},{64,... | collective-permute-start | bytes 294920 | tf_op jit(solution)/shard_map/ppermute | solution.py:419
  22.2 7.1 %collective-permute-start.7 = (f32[64,256]{1,0:T(8,128)S(1)}, f32[64,256]{1,0:T(8,128)S(1)}, u32[]{:S(2)}, u32[]{:S(2)}) collective-permute-start(f32[64,256]{1,0:T(8,128)S(1)} %slice.190), channel_id=1, source_target_pairs={{0,8},{1,9},{2,10},{3,11},{4,12},{5,13},{6,14},{7,15},{8,0},{9,1},... | collective-permute-start | bytes 196616 | tf_op jit(solution)/shard_map/ppermute | solution.py:383
  22.3 7.1 %collective-permute-start.8 = (f32[64,256]{1,0:T(8,128)S(1)}, f32[64,256]{1,0:T(8,128)S(1)}, u32[]{:S(2)}, u32[]{:S(2)}) collective-permute-start(f32[64,256]{1,0:T(8,128)S(1)} %slice.190), channel_id=1, source_target_pairs={{0,0},{1,16},{2,32},{3,48},{4,64},{5,80},{6,96},{7,112},{8,128},{9... | collective-permute-start | bytes 196616 | tf_op jit(solution)/shard_map/ppermute | solution.py:387
  30.7 35.5 %all-to-all-start = ((f32[16,96,256]{2,1,0:T(8,128)}), f32[16,96,256]{2,1,0:T(8,128)S(1)}, u32[]{:S(2)}, u32[]{:S(2)}) async-start(f32[16,96,256]{2,1,0:T(8,128)} %broadcast_in_dim.19), calls=%async_computation | async-start | bytes 3145728 | tf_op jit(solution)/shard_map/all_to_all | solution.py:426
  46.6 5.1 %collective-permute-start.9 = (f32[128,256]{1,0:T(8,128)S(1)}, f32[128,256]{1,0:T(8,128)S(1)}, u32[]{:S(2)}, u32[]{:S(2)}) collective-permute-start(f32[128,256]{1,0:T(8,128)S(1)} %pad_maximum_fusion), channel_id=1, source_target_pairs={{0,2},{1,3},{2,0},{3,1},{4,6},{5,7},{6,4},{7,5},{8,10},{9,11},{10,... | collective-permute-start | bytes 393224 | tf_op jit(solution)/shard_map/ppermute | solution.py:383
  46.8 26.7 %copy-start.10 = (f32[2,1,256,256]{3,2,1,0:T(8,128)}, f32[2,1,256,256]{3,2,1,0:T(8,128)S(1)}, u32[]{:S(2)}) copy-start(f32[2,1,256,256]{3,2,1,0:T(8,128)S(1)} %constant_dynamic-slice_fusion) | copy-start | bytes 1572868
  46.8 16.1 %collective-permute-start.11 = (f32[128,256]{1,0:T(8,128)S(1)}, f32[128,256]{1,0:T(8,128)S(1)}, u32[]{:S(2)}, u32[]{:S(2)}) collective-permute-start(f32[128,256]{1,0:T(8,128)S(1)} %pad_maximum_fusion), channel_id=1, source_target_pairs={{0,6},{1,7},{2,4},{3,5},{4,2},{5,3},{6,0},{7,1},{8,14},{9,15},{10,... | collective-permute-start | bytes 393224 | tf_op jit(solution)/shard_map/ppermute | solution.py:383
  50.8 11.4 %collective-permute-start.10 = (f32[128,256]{1,0:T(8,128)S(1)}, f32[128,256]{1,0:T(8,128)S(1)}, u32[]{:S(2)}, u32[]{:S(2)}) collective-permute-start(f32[128,256]{1,0:T(8,128)S(1)} %pad_maximum_fusion), channel_id=1, source_target_pairs={{0,4},{1,5},{2,6},{3,7},{4,0},{5,1},{6,2},{7,3},{8,12},{9,13},{10,... | collective-permute-start | bytes 393224 | tf_op jit(solution)/shard_map/ppermute | solution.py:383
  63.6 9.9 %collective-permute-start.12 = (f32[512,256]{1,0:T(8,128)}, f32[512,256]{1,0:T(8,128)}, u32[]{:S(2)}, u32[]{:S(2)}) collective-permute-start(f32[512,256]{1,0:T(8,128)} %constant_dynamic-update-slice_fusion.own), channel_id=1, source_target_pairs={{0,1},{1,0},{2,3},{3,2},{4,5},{5,4},{6,7},{7,6},{8,9},{9,8},{10,11... | collective-permute-start | bytes 1572872 | tf_op jit(solution)/shard_map/ppermute | solution.py:383
  65.2 8.2 %collective-permute-start.13 = (f32[512,256]{1,0:T(8,128)S(1)}, f32[512,256]{1,0:T(8,128)S(1)}, u32[]{:S(2)}, u32[]{:S(2)}) collective-permute-start(f32[512,256]{1,0:T(8,128)S(1)} %bitcast.63), channel_id=1, source_target_pairs={{0,1},{1,0},{2,3},{3,2},{4,5},{5,4},{6,7},{7,6},{8,9},{9,8},{10,11... | collective-permute-start | bytes 1572872 | tf_op jit(solution)/shard_map/ppermute | solution.py:383
  66.2 7.3 %copy-start.9 = (f32[16,96,256]{2,1,0:T(8,128)}, f32[16,96,256]{2,1,0:T(8,128)S(1)}, u32[]{:S(2)}) copy-start(f32[16,96,256]{2,1,0:T(8,128)S(1)} %all-to-all-done.cols) | copy-start | bytes 4718596
  67.1 20.7 %all-to-all-start.2 = ((f32[8,64,256]{2,1,0:T(8,128)}), f32[8,64,256]{2,1,0:T(8,128)S(1)}, u32[]{:S(2)}, u32[]{:S(2)}) async-start(f32[8,64,256]{2,1,0:T(8,128)} %broadcast_in_dim.20), calls=%async_computation.2 | async-start | bytes 1048576 | tf_op jit(solution)/shard_map/all_to_all | solution.py:432
  73.5 0.8 copy-start.11
  82.8 10.6 %collective-permute-start.14 = (f32[4,2,112,256]{3,2,1,0:T(8,128)}, f32[4,2,112,256]{3,2,1,0:T(8,128)}, u32[]{:S(2)}, u32[]{:S(2)}) collective-permute-start(f32[4,2,112,256]{3,2,1,0:T(8,128)} %get-tuple-element.56), channel_id=1, source_target_pairs={{0,1},{1,0},{2,3},{3,2},{4,5},{5,4},{6,7},{7,6},{8,9},{9,8},{10,11... | collective-permute-start | bytes 2752520 | tf_op jit(solution)/shard_map/ppermute | solution.py:383
  87.9 29.3 %all-to-all-start.1 = ((f32[16,88,256]{2,1,0:T(8,128)}), f32[16,88,256]{2,1,0:T(8,128)S(1)}, u32[]{:S(2)}, u32[]{:S(2)}) async-start(f32[16,88,256]{2,1,0:T(8,128)} %get-tuple-element.54), calls=%async_computation.1 | async-start | bytes 2883584 | tf_op jit(solution)/shard_map/all_to_all | solution.py:436
  93.3 10.7 %copy-start.8 = (s32[14]{0:T(128)S(1)}, s32[14]{0:T(128)}, u32[]{:S(2)}) copy-start(s32[14]{0:T(128)} %concatenate.36.info) | copy-start | bytes 172
  95.1 7.4 %collective-permute-start.18 = (f32[8,64,256]{2,1,0:T(8,128)S(1)}, f32[8,64,256]{2,1,0:T(8,128)S(1)}, u32[]{:S(2)}, u32[]{:S(2)}) collective-permute-start(f32[8,64,256]{2,1,0:T(8,128)S(1)} %all-to-all-done.2.own), channel_id=1, source_target_pairs={{0,1},{1,0},{2,3},{3,2},{4,5},{5,4},{6,7},{7,6},{8,9},{9,8},{10,11... | collective-permute-start | bytes 1572872 | tf_op jit(solution)/shard_map/ppermute | solution.py:383
  97.9 18.2 %collective-permute-start.15 = (f32[2,112,256]{2,1,0:T(8,128)S(1)}, f32[2,112,256]{2,1,0:T(8,128)S(1)}, u32[]{:S(2)}, u32[]{:S(2)}) collective-permute-start(f32[2,112,256]{2,1,0:T(8,128)S(1)} %get-tuple-element.58), channel_id=1, source_target_pairs={{0,2},{1,3},{2,0},{3,1},{4,6},{5,7},{6,4},{7,5},{8,10},{9,11},{10,... | collective-permute-start | bytes 688136 | tf_op jit(solution)/shard_map/ppermute | solution.py:383
  98.2 17.9 %collective-permute-start.16 = (f32[2,112,256]{2,1,0:T(8,128)S(1)}, f32[2,112,256]{2,1,0:T(8,128)S(1)}, u32[]{:S(2)}, u32[]{:S(2)}) collective-permute-start(f32[2,112,256]{2,1,0:T(8,128)S(1)} %get-tuple-element.59), channel_id=1, source_target_pairs={{0,4},{1,5},{2,6},{3,7},{4,0},{5,1},{6,2},{7,3},{8,12},{9,13},{10,... | collective-permute-start | bytes 688136 | tf_op jit(solution)/shard_map/ppermute | solution.py:383
  98.2 18.0 %collective-permute-start.17 = (f32[2,112,256]{2,1,0:T(8,128)S(1)}, f32[2,112,256]{2,1,0:T(8,128)S(1)}, u32[]{:S(2)}, u32[]{:S(2)}) collective-permute-start(f32[2,112,256]{2,1,0:T(8,128)S(1)} %get-tuple-element.60), channel_id=1, source_target_pairs={{0,6},{1,7},{2,4},{3,5},{4,2},{5,3},{6,0},{7,1},{8,14},{9,15},{10,... | collective-permute-start | bytes 688136 | tf_op jit(solution)/shard_map/ppermute | solution.py:383
  102.5 21.9 %collective-permute-start.20 = (f32[256,256]{1,0:T(8,128)S(1)}, f32[256,256]{1,0:T(8,128)}, u32[]{:S(2)}, u32[]{:S(2)}) collective-permute-start(f32[256,256]{1,0:T(8,128)S(1)} %slice_bitcast_fusion.1), channel_id=1, source_target_pairs={{16,0},{17,1},{18,2},{19,3},{20,4},{21,5},{22,6},{23,7},{24,8},{25... | collective-permute-start | bytes 786440 | tf_op jit(solution)/shard_map/ppermute | solution.py:444
  116.1 0.7 copy-start.3
  116.1 40.2 %copy-start.1 = (f32[256,256]{1,0:T(8,128)}, f32[256,256]{1,0:T(8,128)S(1)}, u32[]{:S(2)}) copy-start(f32[256,256]{1,0:T(8,128)S(1)} %get-tuple-element.79.v0_ref.v0) | copy-start | bytes 786436
  116.2 40.2 %copy-start.2 = (f32[256,256]{1,0:T(8,128)}, f32[256,256]{1,0:T(8,128)S(1)}, u32[]{:S(2)}) copy-start(f32[256,256]{1,0:T(8,128)S(1)} %get-tuple-element.80.p_ref.p01) | copy-start | bytes 786436
  116.8 7.5 %collective-permute-start.19 = (f32[112,256]{1,0:T(8,128)S(1)}, f32[112,256]{1,0:T(8,128)S(1)}, u32[]{:S(2)}, u32[]{:S(2)}) collective-permute-start(f32[112,256]{1,0:T(8,128)S(1)} %get-tuple-element.129), channel_id=1, source_target_pairs={{0,8},{1,9},{2,10},{3,11},{4,12},{5,13},{6,14},{7,15},{8,0},{9,1},... | collective-permute-start | bytes 344072 | tf_op jit(solution)/shard_map/ppermute | solution.py:383
  125.5 37.9 %all-to-all-start.3 = ((f32[16,72,256]{2,1,0:T(8,128)}), f32[16,72,256]{2,1,0:T(8,128)S(1)}, u32[]{:S(2)}, u32[]{:S(2)}) async-start(f32[16,72,256]{2,1,0:T(8,128)} %get-tuple-element.73), calls=%async_computation.3 | async-start | bytes 2359296 | tf_op jit(solution)/shard_map/all_to_all | solution.py:451
  133.6 43.2 %copy-start.12 = (f32[256,256]{1,0:T(8,128)}, f32[256,256]{1,0:T(8,128)S(1)}, u32[]{:S(2)}) copy-start(f32[256,256]{1,0:T(8,128)S(1)} %broadcast_select_fusion.ea) | copy-start | bytes 786436
  133.6 29.8 %collective-permute-start.22 = (f32[256,256]{1,0:T(8,128)S(1)}, f32[256,256]{1,0:T(8,128)}, u32[]{:S(2)}, u32[]{:S(2)}) collective-permute-start(f32[256,256]{1,0:T(8,128)S(1)} %broadcast_select_fusion.ea), channel_id=1, source_target_pairs={{0,1},{1,0},{2,3},{3,2},{4,5},{5,4},{6,7},{7,6},{8,9},{9,8},{10,11... | collective-permute-start | bytes 786440 | tf_op jit(solution)/shard_map/ppermute | solution.py:383
  136.2 20.1 %collective-permute-start.21 = (f32[64,256]{1,0:T(8,128)S(1)}, f32[64,256]{1,0:T(8,128)S(1)}, u32[]{:S(2)}, u32[]{:S(2)}) collective-permute-start(f32[64,256]{1,0:T(8,128)S(1)} %get-tuple-element.74), channel_id=1, source_target_pairs={{0,0},{1,16},{2,32},{3,48},{4,64},{5,80},{6,96},{7,112},{8,128},{9... | collective-permute-start | bytes 196616 | tf_op jit(solution)/shard_map/ppermute | solution.py:387
  162.0 0.7 copy-start.4
  162.8 0.7 copy-start.5
  163.4 6.6 %copy-start.6 = (f32[256,256]{1,0:T(8,128)}, f32[256,256]{1,0:T(8,128)S(1)}, u32[]{:S(2)}) copy-start(f32[256,256]{1,0:T(8,128)S(1)} %get-tuple-element.93.u) | copy-start | bytes 786436
  163.5 28.9 %copy-start.7 = (f32[384,256]{1,0:T(8,128)}, f32[384,256]{1,0:T(8,128)S(1)}, u32[]{:S(2)}) copy-start(f32[384,256]{1,0:T(8,128)S(1)} %get-tuple-element.98.d_own) | copy-start | bytes 1179652
  163.5 17.9 %collective-permute-start.29 = (f32[112,256]{1,0:T(8,128)S(1)}, f32[112,256]{1,0:T(8,128)S(1)}, u32[]{:S(2)}, u32[]{:S(2)}) collective-permute-start(f32[112,256]{1,0:T(8,128)S(1)} %get-tuple-element.97.refs_0_), channel_id=1, source_target_pairs={{14,0},{15,1},{30,16},{31,17},{46,32},{47,33},{62,48},{63,49},{78,... | collective-permute-start | bytes 344072 | tf_op jit(solution)/shard_map/ppermute | solution.py:463
  164.8 17.9 %collective-permute-start.28 = (f32[112,256]{1,0:T(8,128)S(1)}, f32[112,256]{1,0:T(8,128)S(1)}, u32[]{:S(2)}, u32[]{:S(2)}) collective-permute-start(f32[112,256]{1,0:T(8,128)S(1)} %get-tuple-element.97.refs_0_), channel_id=1, source_target_pairs={{12,0},{13,1},{28,16},{29,17},{44,32},{45,33},{60,48},{61,49},{76,... | collective-permute-start | bytes 344072 | tf_op jit(solution)/shard_map/ppermute | solution.py:463
  166.1 17.9 %collective-permute-start.27 = (f32[112,256]{1,0:T(8,128)S(1)}, f32[112,256]{1,0:T(8,128)S(1)}, u32[]{:S(2)}, u32[]{:S(2)}) collective-permute-start(f32[112,256]{1,0:T(8,128)S(1)} %get-tuple-element.97.refs_0_), channel_id=1, source_target_pairs={{10,0},{11,1},{26,16},{27,17},{42,32},{43,33},{58,48},{59,49},{74,... | collective-permute-start | bytes 344072 | tf_op jit(solution)/shard_map/ppermute | solution.py:463
  167.4 16.6 %collective-permute-start.26 = (f32[112,256]{1,0:T(8,128)S(1)}, f32[112,256]{1,0:T(8,128)S(1)}, u32[]{:S(2)}, u32[]{:S(2)}) collective-permute-start(f32[112,256]{1,0:T(8,128)S(1)} %get-tuple-element.97.refs_0_), channel_id=1, source_target_pairs={{8,0},{9,1},{24,16},{25,17},{40,32},{41,33},{56,48},{57,49},{72,64... | collective-permute-start | bytes 344072 | tf_op jit(solution)/shard_map/ppermute | solution.py:463
  168.7 15.4 %collective-permute-start.25 = (f32[112,256]{1,0:T(8,128)S(1)}, f32[112,256]{1,0:T(8,128)S(1)}, u32[]{:S(2)}, u32[]{:S(2)}) collective-permute-start(f32[112,256]{1,0:T(8,128)S(1)} %get-tuple-element.97.refs_0_), channel_id=1, source_target_pairs={{6,0},{7,1},{22,16},{23,17},{38,32},{39,33},{54,48},{55,49},{70,64... | collective-permute-start | bytes 344072 | tf_op jit(solution)/shard_map/ppermute | solution.py:463
  181.5 6.9 %collective-permute-start.24 = (f32[112,256]{1,0:T(8,128)S(1)}, f32[112,256]{1,0:T(8,128)S(1)}, u32[]{:S(2)}, u32[]{:S(2)}) collective-permute-start(f32[112,256]{1,0:T(8,128)S(1)} %get-tuple-element.97.refs_0_), channel_id=1, source_target_pairs={{4,0},{5,1},{20,16},{21,17},{36,32},{37,33},{52,48},{53,49},{68,64... | collective-permute-start | bytes 344072 | tf_op jit(solution)/shard_map/ppermute | solution.py:463
  182.8 9.0 %collective-permute-start.23 = (f32[112,256]{1,0:T(8,128)S(1)}, f32[112,256]{1,0:T(8,128)S(1)}, u32[]{:S(2)}, u32[]{:S(2)}) collective-permute-start(f32[112,256]{1,0:T(8,128)S(1)} %get-tuple-element.97.refs_0_), channel_id=1, source_target_pairs={{2,0},{3,1},{18,16},{19,17},{34,32},{35,33},{50,48},{51,49},{66,64... | collective-permute-start | bytes 344072 | tf_op jit(solution)/shard_map/ppermute | solution.py:463
  191.9 3.3 %copy-start = (f32[896,256]{1,0:T(8,128)}, f32[896,256]{1,0:T(8,128)S(1)}, u32[]{:S(2)}) copy-start(f32[896,256]{1,0:T(8,128)S(1)} %joined.1.mine) | copy-start | bytes 2752516
  191.9 3.2 %collective-permute-start.30 = (f32[896,256]{1,0:T(8,128)S(1)}, f32[896,256]{1,0:T(8,128)S(1)}, u32[]{:S(2)}, u32[]{:S(2)}) collective-permute-start(f32[896,256]{1,0:T(8,128)S(1)} %joined.1.mine), channel_id=1, source_target_pairs={{0,1},{1,0},{2,3},{3,2},{4,5},{5,4},{6,7},{7,6},{8,9},{9,8},{10,11... | collective-permute-start | bytes 2752520 | tf_op jit(solution)/shard_map/ppermute | solution.py:383
  192.4 2.7 %collective-permute-start.31 = (f32[384,256]{1,0:T(8,128)S(1)}, f32[384,256]{1,0:T(8,128)S(1)}, u32[]{:S(2)}, u32[]{:S(2)}) collective-permute-start(f32[384,256]{1,0:T(8,128)S(1)} %get-tuple-element.98.d_own), channel_id=1, source_target_pairs={{0,1},{1,0},{2,3},{3,2},{4,5},{5,4},{6,7},{7,6},{8,9},{9,8},{10,11... | collective-permute-start | bytes 1179656 | tf_op jit(solution)/shard_map/ppermute | solution.py:383
  195.1 0.8 copy-start.14
  195.9 0.9 copy-start.13

commit v2 on v1

--- a/solution.py
+++ b/solution.py
@@ -317,7 +317,7 @@
     return 0.5 * (full + full.T)
 
 
-def grad_kernel(info, cot, mine, other, d_own, d_far, ca, co, ea, eo, v0, v1, u, p01, l0, l1, out):
+def grad_kernel(info, cot, mine, other, d_own, d_far, ca, co, edge, near_edge, far_edge, v0, v1, u, p01, l0, l1, out):
     row, col = info[0], info[1]
     sr = info[2]
     for i in range(3):
@@ -340,6 +340,26 @@
         g0 = dot3(split(e0 - dot3(h0s, w0, NT) - dot3(split(g1), p)), w0)
         zero = jnp.zeros((B, B), f32)
         column = jnp.where(first, g0, g1)
+        t = jnp.concatenate([x[112 * q + 64 : 112 * q + 112] for x in (left, right) for q in range(8)], 0)
+        d0, d1 = d_own[...], d_far[...]
+        d = jnp.concatenate([jnp.where(first, d0, d1), jnp.where(first, d1, d0)], 0)
+        t00, t01, t11 = t[:B], t[B : 2 * B], t[2 * B :]
+        d00, d10, d11 = d[:B], d[B : 2 * B], d[2 * B :]
+        c10 = jnp.where(row == 0, near_edge[...], edge[...])
+        c11 = jnp.where(row == 0, far_edge[...], jnp.where(first, near_edge[...], edge[...]))
+        t00s, t01s = split(t00), split(t01)
+        a10 = split(d10 - dot3(w1, t01s, NT) + dot3(mix, t00s, TN))
+        a11 = split(d11 - dot3(w1, split(t11)) + dot3(mix, t01s, TN))
+        s1 = dot3(a11, w1, NT) - dot3(a10, mix)
+        b1 = pull_cholesky(split(l1[...]), w1, c11 - dot3(w1, split(s1), TN))
+        va = split(dot3(w1, a10, TN))
+        bar10 = split(c10 - 2.0 * dot3(split(b1), p) - dot3(va, w0, NT))
+        s0 = dot3(split(d00 - dot3(w0, t00s) - dot3(p, va, TN)), w0, NT)
+        b0 = pull_cholesky(split(l0[...]), w0, cot[0, 0] - dot3(w0, split(s0 + dot3(bar10, p, TN)), TN))
+        upper = jnp.where(first, b0, zero)
+        lower = jnp.where(first, dot3(bar10, w0), b1)
+        corner = jnp.where(row == 0, upper, lower) * cot_keep(info, 0)
+
         out[0, 0] = zero
         out[2, 0] = zero
         out[sr, 0] = column[:B] * cot_keep(info, sr)
@@ -347,25 +367,7 @@
 
         @pl.when(row < 2)
         def _():
-            t = jnp.concatenate([x[112 * q + 64 : 112 * q + 112] for x in (left, right) for q in range(8)], 0)
-            d0, d1 = d_own[...], d_far[...]
-            d = jnp.concatenate([jnp.where(first, d0, d1), jnp.where(first, d1, d0)], 0)
-            t00, t01, t11 = t[:B], t[B : 2 * B], t[2 * B :]
-            d00, d10, d11 = d[:B], d[B : 2 * B], d[2 * B :]
-            c10 = jnp.where(first, ea[...], eo[...])
-            c11 = jnp.where(first, eo[...], ea[...])
-            t00s, t01s = split(t00), split(t01)
-            a10 = split(d10 - dot3(w1, t01s, NT) + dot3(mix, t00s, TN))
-            a11 = split(d11 - dot3(w1, split(t11)) + dot3(mix, t01s, TN))
-            s1 = dot3(a11, w1, NT) - dot3(a10, mix)
-            b1 = pull_cholesky(split(l1[...]), w1, c11 - dot3(w1, split(s1), TN))
-            va = split(dot3(w1, a10, TN))
-            bar10 = split(c10 - 2.0 * dot3(split(b1), p) - dot3(va, w0, NT))
-            s0 = dot3(split(d00 - dot3(w0, t00s) - dot3(p, va, TN)), w0, NT)
-            b0 = pull_cholesky(split(l0[...]), w0, cot[0, 0] - dot3(w0, split(s0 + dot3(bar10, p, TN)), TN))
-            upper = jnp.where(first, b0, zero)
-            lower = jnp.where(first, dot3(bar10, w0), b1)
-            out[0, 0] = jnp.where(row == 0, upper, lower) * cot_keep(info, 0)
+            out[0, 0] = corner
 
 
 def cot_keep(info, slot):
@@ -440,22 +442,21 @@
     cut_far = flip(cut, "col", 1)
     v0, l0, p01, x1 = corner_call(corner_a_kernel, "corner_a", 4, 3, info, cut, cut_far)
     came = [flip(part[m], "col", 2 * m) for m in range(1, 4)]
-    edge = cot3[0, 0]
-    from_one = lax.ppermute(after(edge, cut_far), "row", [(1, 0)])
+    edge = after(cot3[0, 0], cut_far)
+    near_edge = lax.ppermute(edge, ("row", "col"), [(N, 0), (N + 1, N)])
+    far_edge = lax.ppermute(edge, ("row", "col"), [(N + 1, 0)])
     came, x1 = lax.optimization_barrier((came, x1))
     part = part[0] + came[0] + came[1] + came[2]
     near, came = part[0], flip(part[1], "col", 8)
-    by_col, came, x1, from_one = lax.optimization_barrier((by_col, came, x1, from_one))
+    by_col, came, x1, near_edge, far_edge = lax.optimization_barrier((by_col, came, x1, near_edge, far_edge))
     h_row, h_col, td = sums(by_col, near, came)
     td, x1, h_col = lax.optimization_barrier((td, x1, h_col))
     td = lax.all_to_all(td, "row", 0, 0)
     h_col = transposed(h_col)
-    ea = jnp.where(row == 0, from_one, edge)
-    eo = flip(ea, "col", 1)
     a1, v1 = corner_call(corner_c_kernel, "corner_c", 2, 0, x1)
-    h_col, a1 = lax.optimization_barrier((h_col, a1))
     v1, l1, u = corner_call(corner_d_kernel, "corner_d", 3, 1, a1, v1, v0, p01)
-    td, u, eo, h_col = lax.optimization_barrier((td, u, eo, h_col))
+    h_col, u = lax.optimization_barrier((h_col, u))
+    td, h_col = lax.optimization_barrier((td, h_col))
 
     send, d_half = table_sums(td, h_row, h_col)
     send, xi = lax.optimization_barrier((send, xi))
@@ -469,7 +470,7 @@
     pieces = [send] + [to_owner(again, q) for q in range(1, 3)] + pieces
     mine = joined(pieces)
     theirs = flip(mine, "col", 1)
-    grad_out = grad_of(info, cot3, mine, theirs, d_half, d_far, ca, co, ea, eo, v0, v1, u, p01, l0, l1)
+    grad_out = grad_of(info, cot3, mine, theirs, d_half, d_far, ca, co, edge, near_edge, far_edge, v0, v1, u, p01, l0, l1)
     return (factor_out.reshape(kernel.shape), grad_out.reshape(kernel.shape))
 
 

time: 211 us -> 214 us (1.014)
  the two profiles are of different devices: /device:TPU:1 before, /device:TPU:3 now
where the time goes in v2:
time: 214 us; the launch traced here: 210 us
  starting transfers between devices  102 us (48%)
  Pallas kernels  50.7 us (24%)
  waiting for transfers between devices  40.7 us (19%)
  local copies, waits for them, and re-layouts  11.7 us (5%)
  other arithmetic  4.07 us (2%)
    pallas_call x9, Pallas kernels, run(): pl.pallas_call(body, grid=(1,), out_shape=outputs, in_specs=[SMEM if x.dt...  50.7 us
    ppermute x2, starting transfers between devices, transposed(): lax.ppermute(x, ('row', 'col'), [(r * N + c, c * N + r) for r in range(N)...  31.4 us
    ppermute x14, waiting for transfers between devices, flip(): return lax.ppermute(x, axis, [(i, i ^ m) for i in range(N)])  19.6 us
    ppermute x14, starting transfers between devices, flip(): return lax.ppermute(x, axis, [(i, i ^ m) for i in range(N)])  17.5 us
    ppermute x7, starting transfers between devices, on_device(): lax.ppermute(pieces[q], 'col', [(a, 2 * q + a) for a in range(2)])  14.7 us
    ppermute x7, waiting for transfers between devices, to_owner(): return lax.ppermute(x, 'col', [(2 * q + a, a) for a in range(2)])  11.8 us
    ppermute x7, starting transfers between devices, to_owner(): return lax.ppermute(x, 'col', [(2 * q + a, a) for a in range(2)])  9.03 us
    all_to_all x1, starting transfers between devices, on_device(): cols = lax.all_to_all(jnp.broadcast_to(col_send, (N, 96, B)), 'row', 0, 0)  8.68 us
  transfers between devices with their start and end apart: 36, of which 10 were waited for; matrix products, arithmetic and copies ran while one was open for 4% of the time, Pallas kernels for 18%

profile of v2, /device:TPU:3, one launch (start us, length us, event | category | flops | bytes accessed | tf_op | source)
XLA Modules:
  0.0 210.4 jit_solution(7527128745282963869)
XLA Ops:
  0.7 0.7 fusion.16
  1.6 1.3 fusion
  3.0 3.5 %collective-permute-start = (f32[96,256]{1,0:T(8,128)S(1)}, f32[96,256]{1,0:T(8,128)S(1)}, u32[]{:S(2)}, u32[]{:S(2)}) collective-permute-start(f32[96,256]{1,0:T(8,128)S(1)} %pad_maximum_fusion.1), channel_id=1, source_target_pairs={{0,2},{1,3},{16,18},{17,19},{32,34},{33,35},{48,50},{49,51},{64,66... | collective-permute-start | bytes 294920 | tf_op jit(solution)/shard_map/ppermute | solution.py:421
  6.6 2.0 collective-permute-start.1
  8.6 2.0 collective-permute-start.2
  10.7 3.2 %collective-permute-start.3 = (f32[96,256]{1,0:T(8,128)S(1)}, f32[96,256]{1,0:T(8,128)S(1)}, u32[]{:S(2)}, u32[]{:S(2)}) collective-permute-start(f32[96,256]{1,0:T(8,128)S(1)} %pad_maximum_fusion.4), channel_id=1, source_target_pairs={{0,8},{1,9},{16,24},{17,25},{32,40},{33,41},{48,56},{49,57},{64,72... | collective-permute-start | bytes 294920 | tf_op jit(solution)/shard_map/ppermute | solution.py:421
  13.9 1.3 collective-permute-start.4
  15.3 1.3 collective-permute-start.5
  16.6 1.3 collective-permute-start.6
  17.9 1.2 collective-permute-done.5
  19.2 2.1 %collective-permute-done.6 = f32[96,256]{1,0:T(8,128)S(1)} collective-permute-done((f32[96,256]{1,0:T(8,128)S(1)}, f32[96,256]{1,0:T(8,128)S(1)}, u32[]{:S(2)}, u32[]{:S(2)}) %collective-permute-start.6) | collective-permute-done | bytes 98336 | tf_op jit(solution)/shard_map/ppermute | solution.py:421
  21.4 9.4 %collective-permute-start.8 = (f32[64,256]{1,0:T(8,128)S(1)}, f32[64,256]{1,0:T(8,128)S(1)}, u32[]{:S(2)}, u32[]{:S(2)}) collective-permute-start(f32[64,256]{1,0:T(8,128)S(1)} %slice.190), channel_id=1, source_target_pairs={{0,0},{1,16},{2,32},{3,48},{4,64},{5,80},{6,96},{7,112},{8,128},{9... | collective-permute-start | bytes 196616 | tf_op jit(solution)/shard_map/ppermute | solution.py:389
  30.9 3.9 %collective-permute-done.8 = f32[64,256]{1,0:T(8,128)S(1)} collective-permute-done((f32[64,256]{1,0:T(8,128)S(1)}, f32[64,256]{1,0:T(8,128)S(1)}, u32[]{:S(2)}, u32[]{:S(2)}) %collective-permute-start.8) | collective-permute-done | bytes 65568 | tf_op jit(solution)/shard_map/ppermute | solution.py:389
  34.8 1.3 broadcast_in_dim.19
  36.1 8.7 %all-to-all-start = ((f32[16,96,256]{2,1,0:T(8,128)}), f32[16,96,256]{2,1,0:T(8,128)S(1)}, u32[]{:S(2)}, u32[]{:S(2)}) async-start(f32[16,96,256]{2,1,0:T(8,128)} %broadcast_in_dim.19), calls=%async_computation | async-start | bytes 3145728 | tf_op jit(solution)/shard_map/all_to_all | solution.py:428
  44.8 1.2 slice.192
  46.1 4.0 %collective-permute-start.11 = (f32[128,256]{1,0:T(8,128)S(1)}, f32[128,256]{1,0:T(8,128)S(1)}, u32[]{:S(2)}, u32[]{:S(2)}) collective-permute-start(f32[128,256]{1,0:T(8,128)S(1)} %pad_maximum_fusion), channel_id=1, source_target_pairs={{0,6},{1,7},{2,4},{3,5},{4,2},{5,3},{6,0},{7,1},{8,14},{9,15},{10,... | collective-permute-start | bytes 393224 | tf_op jit(solution)/shard_map/ppermute | solution.py:385
  50.4 0.7 constant_dynamic-update-slice_fusion.3
  51.1 0.7 constant_dynamic-update-slice_fusion.2
  51.7 9.8 %collective-permute-done.10 = f32[128,256]{1,0:T(8,128)S(1)} collective-permute-done((f32[128,256]{1,0:T(8,128)S(1)}, f32[128,256]{1,0:T(8,128)S(1)}, u32[]{:S(2)}, u32[]{:S(2)}) %collective-permute-start.10) | collective-permute-done | bytes 131104 | tf_op jit(solution)/shard_map/ppermute | solution.py:385
  61.5 0.6 constant_dynamic-update-slice_fusion.1
  62.2 0.6 constant_dynamic-update-slice_fusion.own
  62.8 1.7 collective-permute-start.12
  64.9 0.6 concatenate.36.info
  65.5 0.9 broadcast_in_dim.20
  66.4 3.6 %all-to-all-start.2 = ((f32[8,64,256]{2,1,0:T(8,128)}), f32[8,64,256]{2,1,0:T(8,128)S(1)}, u32[]{:S(2)}, u32[]{:S(2)}) async-start(f32[8,64,256]{2,1,0:T(8,128)} %broadcast_in_dim.20), calls=%async_computation.2 | async-start | bytes 1048576 | tf_op jit(solution)/shard_map/all_to_all | solution.py:434
  70.0 8.5 %partials.1 = (f32[2,512,256]{2,1,0:T(8,128)}, f32[2,512,256]{2,1,0:T(8,128)}, f32[4,2,112,256]{3,2,1,0:T(8,128)}, f32[4,2,112,256]{3,2,1,0:T(8,128)}, f32[16,88,256]{2,1,0:T(8,128)}) custom-call(s32[14]{0:T(128)} %concatenate.36.info, f32[3,3,256,256]{3,2,1,0:T(8,128)} %bitcast.57, f32[512,256]{1,0:T(8,128)} %constant_dynamic-update-slice_fusion.own, ...), custom_call_target="tpu_custom_call" | custom-call | tf_op jit(solution)/shard_map/partials/pallas_call | solution.py:93
  78.5 3.6 %collective-permute-start.14 = (f32[4,2,112,256]{3,2,1,0:T(8,128)}, f32[4,2,112,256]{3,2,1,0:T(8,128)}, u32[]{:S(2)}, u32[]{:S(2)}) collective-permute-start(f32[4,2,112,256]{3,2,1,0:T(8,128)} %get-tuple-element.55), channel_id=1, source_target_pairs={{0,1},{1,0},{2,3},{3,2},{4,5},{5,4},{6,7},{7,6},{8,9},{9,8},{10,11... | collective-permute-start | bytes 2752520 | tf_op jit(solution)/shard_map/ppermute | solution.py:385
  82.1 2.0 all-to-all-done.2.own
  84.1 8.4 %all-to-all-start.1 = ((f32[16,88,256]{2,1,0:T(8,128)}), f32[16,88,256]{2,1,0:T(8,128)S(1)}, u32[]{:S(2)}, u32[]{:S(2)}) async-start(f32[16,88,256]{2,1,0:T(8,128)} %get-tuple-element.53), calls=%async_computation.1 | async-start | bytes 2883584 | tf_op jit(solution)/shard_map/all_to_all | solution.py:438
  92.6 1.7 fusion.1
  94.3 3.2 %collective-permute-start.18 = (f32[8,64,256]{2,1,0:T(8,128)S(1)}, f32[8,64,256]{2,1,0:T(8,128)S(1)}, u32[]{:S(2)}, u32[]{:S(2)}) collective-permute-start(f32[8,64,256]{2,1,0:T(8,128)S(1)} %all-to-all-done.2.own), channel_id=1, source_target_pairs={{0,1},{1,0},{2,3},{3,2},{4,5},{5,4},{6,7},{7,6},{8,9},{9,8},{10,11... | collective-permute-start | bytes 1572872 | tf_op jit(solution)/shard_map/ppermute | solution.py:385
  97.5 0.3 collective-permute-start.15
  97.8 3.3 %collective-permute-start.17 = (f32[2,112,256]{2,1,0:T(8,128)S(1)}, f32[2,112,256]{2,1,0:T(8,128)S(1)}, u32[]{:S(2)}, u32[]{:S(2)}) collective-permute-start(f32[2,112,256]{2,1,0:T(8,128)S(1)} %get-tuple-element.59), channel_id=1, source_target_pairs={{0,6},{1,7},{2,4},{3,5},{4,2},{5,3},{6,0},{7,1},{8,14},{9,15},{10,... | collective-permute-start | bytes 688136 | tf_op jit(solution)/shard_map/ppermute | solution.py:385
  101.0 1.0 slice_bitcast_fusion.1.edge
  102.0 0.7 collective-permute-start.21
  102.7 0.9 collective-permute-start.20
  103.7 12.1 %corner_a.1 = (f32[256,256]{1,0:T(8,128)S(1)}, f32[256,256]{1,0:T(8,128)S(1)}, f32[256,256]{1,0:T(8,128)S(1)}, f32[256,256]{1,0:T(8,128)S(1)}) custom-call(s32[14]{0:T(128)S(1)} %copy-done.8, f32[8,64,256]{2,1,0:T(8,128)S(1)} %all-to-all-done.2.own, f32[8,64,256]{2,1,0:T(8,128)S(1)} %collective-permute-done.18.far), custom_call_target="tpu_custom_call" | custom-call | tf_op jit(solution)/shard_map/corner_a/pallas_call | solution.py:93
  115.9 0.6 copy-done.3
  116.5 0.3 collective-permute-start.19
  116.8 7.3 %collective-permute-done.19.came = f32[112,256]{1,0:T(8,128)S(1)} collective-permute-done((f32[112,256]{1,0:T(8,128)S(1)}, f32[112,256]{1,0:T(8,128)S(1)}, u32[]{:S(2)}, u32[]{:S(2)}) %collective-permute-start.19) | collective-permute-done | bytes 114720 | tf_op jit(solution)/shard_map/ppermute | solution.py:385
  124.0 1.2 sums.1
  125.2 6.7 %all-to-all-start.3 = ((f32[16,72,256]{2,1,0:T(8,128)}), f32[16,72,256]{2,1,0:T(8,128)S(1)}, u32[]{:S(2)}, u32[]{:S(2)}) async-start(f32[16,72,256]{2,1,0:T(8,128)} %get-tuple-element.72), calls=%async_computation.3 | async-start | bytes 2359296 | tf_op jit(solution)/shard_map/all_to_all | solution.py:454
  131.9 22.0 %collective-permute-start.22 = (f32[64,256]{1,0:T(8,128)S(1)}, f32[64,256]{1,0:T(8,128)S(1)}, u32[]{:S(2)}, u32[]{:S(2)}) collective-permute-start(f32[64,256]{1,0:T(8,128)S(1)} %get-tuple-element.73), channel_id=1, source_target_pairs={{0,0},{1,16},{2,32},{3,48},{4,64},{5,80},{6,96},{7,112},{8,128},{9... | collective-permute-start | bytes 196616 | tf_op jit(solution)/shard_map/ppermute | solution.py:389
  153.9 5.5 %corner_c.1 = (f32[256,256]{1,0:T(8,128)S(1)}, f32[256,256]{1,0:T(8,128)S(1)}) custom-call(f32[256,256]{1,0:T(8,128)S(1)} %get-tuple-element.74.x_ref), custom_call_target="tpu_custom_call" | custom-call | tf_op jit(solution)/shard_map/corner_c/pallas_call | solution.py:93
  159.4 5.6 %corner_d.1 = (f32[256,256]{1,0:T(8,128)S(1)}, f32[256,256]{1,0:T(8,128)S(1)}, f32[256,256]{1,0:T(8,128)S(1)}) custom-call(f32[256,256]{1,0:T(8,128)S(1)} %get-tuple-element.75.a_in, f32[256,256]{1,0:T(8,128)S(1)} %get-tuple-element.76.v_in, f32[256,256]{1,0:T(8,128)S(1)} %get-tuple-element.77.v0_ref.v0, f32[256,256]{1,0:T(8,128)S(1)} %get-tuple-element.78.p_ref.p01), custom_call_target="tpu_custom_call" | custom-call | tf_op jit(solution)/shard_map/corner_d/pallas_call | solution.py:93
  165.1 0.7 copy-done.4
  165.8 0.7 copy-done.5
  166.6 1.3 collective-permute-start.29
  167.9 1.3 collective-permute-start.28
  169.2 1.3 collective-permute-start.27
  170.5 1.3 collective-permute-start.26
  171.8 1.3 collective-permute-start.25
  173.1 6.7 %factor.1 = f32[3,3,256,256]{3,2,1,0:T(8,128)} custom-call(s32[14]{0:T(128)} %concatenate.36.info, f32[3,3,256,256]{3,2,1,0:T(8,128)} %bitcast.64, f32[2,512,256]{2,1,0:T(8,128)} %get-tuple-element.87.xi, f32[2,512,256]{2,1,0:T(8,128)} %get-tuple-element.88.xj, f32[256,256]{1,0:T(8,128)} %copy-done.1, f32[256,256]{1,0:T(8,128)} %copy-done.4, ...), custom_call_target="tpu_custom_call" | custom-call | tf_op jit(solution)/shard_map/factor/pallas_call | solution.py:93
  179.8 4.1 %collective-permute-done.29.refs_7_ = f32[112,256]{1,0:T(8,128)S(1)} collective-permute-done((f32[112,256]{1,0:T(8,128)S(1)}, f32[112,256]{1,0:T(8,128)S(1)}, u32[]{:S(2)}, u32[]{:S(2)}) %collective-permute-start.29) | collective-permute-done | bytes 114720 | tf_op jit(solution)/shard_map/ppermute | solution.py:464
  183.9 1.3 collective-permute-start.24
  185.2 1.3 collective-permute-start.23
  186.5 4.3 %collective-permute-done.24.refs_2_ = f32[112,256]{1,0:T(8,128)S(1)} collective-permute-done((f32[112,256]{1,0:T(8,128)S(1)}, f32[112,256]{1,0:T(8,128)S(1)}, u32[]{:S(2)}, u32[]{:S(2)}) %collective-permute-start.24) | collective-permute-done | bytes 114720 | tf_op jit(solution)/shard_map/ppermute | solution.py:464
  190.9 3.4 %collective-permute-done.23.refs_1_ = f32[112,256]{1,0:T(8,128)S(1)} collective-permute-done((f32[112,256]{1,0:T(8,128)S(1)}, f32[112,256]{1,0:T(8,128)S(1)}, u32[]{:S(2)}, u32[]{:S(2)}) %collective-permute-start.23) | collective-permute-done | bytes 114720 | tf_op jit(solution)/shard_map/ppermute | solution.py:464
  194.3 0.6 collective-permute-start.30
  195.0 2.6 %collective-permute-done.31.d_far = f32[384,256]{1,0:T(8,128)S(1)} collective-permute-done((f32[384,256]{1,0:T(8,128)S(1)}, f32[384,256]{1,0:T(8,128)S(1)}, u32[]{:S(2)}, u32[]{:S(2)}) %collective-permute-start.31) | collective-permute-done | bytes 393248 | tf_op jit(solution)/shard_map/ppermute | solution.py:385
  197.5 0.7 copy-done.13
  198.3 0.9 copy-done.12
  199.2 11.0 %grad.1 = f32[3,3,256,256]{3,2,1,0:T(8,128)} custom-call(s32[14]{0:T(128)} %concatenate.36.info, f32[3,3,256,256]{3,2,1,0:T(8,128)} %bitcast.59, f32[896,256]{1,0:T(8,128)} %copy-done, f32[896,256]{1,0:T(8,128)} %copy-done.12, f32[384,256]{1,0:T(8,128)} %copy-done.7, f32[384,256]{1,0:T(8,128)} %copy-done.13, f32[512,256]{1,0:T(8,128)} %bitcast.62, ...), custom_call_target="tpu_custom_call" | custom-call | tf_op jit(solution)/shard_map/grad/pallas_call | solution.py:93
  (89 shorter events, 1.8 us)
Async XLA Ops:
  3.0 12.3 %collective-permute-start = (f32[96,256]{1,0:T(8,128)S(1)}, f32[96,256]{1,0:T(8,128)S(1)}, u32[]{:S(2)}, u32[]{:S(2)}) collective-permute-start(f32[96,256]{1,0:T(8,128)S(1)} %pad_maximum_fusion.1), channel_id=1, source_target_pairs={{0,2},{1,3},{16,18},{17,19},{32,34},{33,35},{48,50},{49,51},{64,66... | collective-permute-start | bytes 294920 | tf_op jit(solution)/shard_map/ppermute | solution.py:421
  6.6 10.0 %collective-permute-start.1 = (f32[96,256]{1,0:T(8,128)S(1)}, f32[96,256]{1,0:T(8,128)S(1)}, u32[]{:S(2)}, u32[]{:S(2)}) collective-permute-start(f32[96,256]{1,0:T(8,128)S(1)} %pad_maximum_fusion.2), channel_id=1, source_target_pairs={{0,4},{1,5},{16,20},{17,21},{32,36},{33,37},{48,52},{49,53},{64,68... | collective-permute-start | bytes 294920 | tf_op jit(solution)/shard_map/ppermute | solution.py:421
  8.6 9.3 %collective-permute-start.2 = (f32[96,256]{1,0:T(8,128)S(1)}, f32[96,256]{1,0:T(8,128)S(1)}, u32[]{:S(2)}, u32[]{:S(2)}) collective-permute-start(f32[96,256]{1,0:T(8,128)S(1)} %pad_maximum_fusion.3), channel_id=1, source_target_pairs={{0,6},{1,7},{16,22},{17,23},{32,38},{33,39},{48,54},{49,55},{64,70... | collective-permute-start | bytes 294920 | tf_op jit(solution)/shard_map/ppermute | solution.py:421
  10.7 7.2 %collective-permute-start.3 = (f32[96,256]{1,0:T(8,128)S(1)}, f32[96,256]{1,0:T(8,128)S(1)}, u32[]{:S(2)}, u32[]{:S(2)}) collective-permute-start(f32[96,256]{1,0:T(8,128)S(1)} %pad_maximum_fusion.4), channel_id=1, source_target_pairs={{0,8},{1,9},{16,24},{17,25},{32,40},{33,41},{48,56},{49,57},{64,72... | collective-permute-start | bytes 294920 | tf_op jit(solution)/shard_map/ppermute | solution.py:421
  13.9 4.0 %collective-permute-start.4 = (f32[96,256]{1,0:T(8,128)S(1)}, f32[96,256]{1,0:T(8,128)S(1)}, u32[]{:S(2)}, u32[]{:S(2)}) collective-permute-start(f32[96,256]{1,0:T(8,128)S(1)} %pad_maximum_fusion.5), channel_id=1, source_target_pairs={{0,10},{1,11},{16,26},{17,27},{32,42},{33,43},{48,58},{49,59},{64,... | collective-permute-start | bytes 294920 | tf_op jit(solution)/shard_map/ppermute | solution.py:421
  15.3 3.9 %collective-permute-start.5 = (f32[96,256]{1,0:T(8,128)S(1)}, f32[96,256]{1,0:T(8,128)S(1)}, u32[]{:S(2)}, u32[]{:S(2)}) collective-permute-start(f32[96,256]{1,0:T(8,128)S(1)} %pad_maximum_fusion.6), channel_id=1, source_target_pairs={{0,12},{1,13},{16,28},{17,29},{32,44},{33,45},{48,60},{49,61},{64,... | collective-permute-start | bytes 294920 | tf_op jit(solution)/shard_map/ppermute | solution.py:421
  16.6 4.7 %collective-permute-start.6 = (f32[96,256]{1,0:T(8,128)S(1)}, f32[96,256]{1,0:T(8,128)S(1)}, u32[]{:S(2)}, u32[]{:S(2)}) collective-permute-start(f32[96,256]{1,0:T(8,128)S(1)} %pad_maximum_fusion.7), channel_id=1, source_target_pairs={{0,14},{1,15},{16,30},{17,31},{32,46},{33,47},{48,62},{49,63},{64,... | collective-permute-start | bytes 294920 | tf_op jit(solution)/shard_map/ppermute | solution.py:421
  21.3 9.5 %collective-permute-start.7 = (f32[64,256]{1,0:T(8,128)S(1)}, f32[64,256]{1,0:T(8,128)S(1)}, u32[]{:S(2)}, u32[]{:S(2)}) collective-permute-start(f32[64,256]{1,0:T(8,128)S(1)} %slice.190), channel_id=1, source_target_pairs={{0,8},{1,9},{2,10},{3,11},{4,12},{5,13},{6,14},{7,15},{8,0},{9,1},... | collective-permute-start | bytes 196616 | tf_op jit(solution)/shard_map/ppermute | solution.py:385
  21.4 13.3 %collective-permute-start.8 = (f32[64,256]{1,0:T(8,128)S(1)}, f32[64,256]{1,0:T(8,128)S(1)}, u32[]{:S(2)}, u32[]{:S(2)}) collective-permute-start(f32[64,256]{1,0:T(8,128)S(1)} %slice.190), channel_id=1, source_target_pairs={{0,0},{1,16},{2,32},{3,48},{4,64},{5,80},{6,96},{7,112},{8,128},{9... | collective-permute-start | bytes 196616 | tf_op jit(solution)/shard_map/ppermute | solution.py:389
  36.1 29.4 %all-to-all-start = ((f32[16,96,256]{2,1,0:T(8,128)}), f32[16,96,256]{2,1,0:T(8,128)S(1)}, u32[]{:S(2)}, u32[]{:S(2)}) async-start(f32[16,96,256]{2,1,0:T(8,128)} %broadcast_in_dim.19), calls=%async_computation | async-start | bytes 3145728 | tf_op jit(solution)/shard_map/all_to_all | solution.py:428
  46.0 5.1 %collective-permute-start.9 = (f32[128,256]{1,0:T(8,128)S(1)}, f32[128,256]{1,0:T(8,128)S(1)}, u32[]{:S(2)}, u32[]{:S(2)}) collective-permute-start(f32[128,256]{1,0:T(8,128)S(1)} %pad_maximum_fusion), channel_id=1, source_target_pairs={{0,2},{1,3},{2,0},{3,1},{4,6},{5,7},{6,4},{7,5},{8,10},{9,11},{10,... | collective-permute-start | bytes 393224 | tf_op jit(solution)/shard_map/ppermute | solution.py:385
  46.1 23.9 %copy-start.10 = (f32[2,1,256,256]{3,2,1,0:T(8,128)}, f32[2,1,256,256]{3,2,1,0:T(8,128)S(1)}, u32[]{:S(2)}) copy-start(f32[2,1,256,256]{3,2,1,0:T(8,128)S(1)} %constant_dynamic-slice_fusion) | copy-start | bytes 1572868
  46.1 16.1 %collective-permute-start.11 = (f32[128,256]{1,0:T(8,128)S(1)}, f32[128,256]{1,0:T(8,128)S(1)}, u32[]{:S(2)}, u32[]{:S(2)}) collective-permute-start(f32[128,256]{1,0:T(8,128)S(1)} %pad_maximum_fusion), channel_id=1, source_target_pairs={{0,6},{1,7},{2,4},{3,5},{4,2},{5,3},{6,0},{7,1},{8,14},{9,15},{10,... | collective-permute-start | bytes 393224 | tf_op jit(solution)/shard_map/ppermute | solution.py:385
  50.2 11.4 %collective-permute-start.10 = (f32[128,256]{1,0:T(8,128)S(1)}, f32[128,256]{1,0:T(8,128)S(1)}, u32[]{:S(2)}, u32[]{:S(2)}) collective-permute-start(f32[128,256]{1,0:T(8,128)S(1)} %pad_maximum_fusion), channel_id=1, source_target_pairs={{0,4},{1,5},{2,6},{3,7},{4,0},{5,1},{6,2},{7,3},{8,12},{9,13},{10,... | collective-permute-start | bytes 393224 | tf_op jit(solution)/shard_map/ppermute | solution.py:385
  62.8 7.2 %collective-permute-start.12 = (f32[512,256]{1,0:T(8,128)}, f32[512,256]{1,0:T(8,128)}, u32[]{:S(2)}, u32[]{:S(2)}) collective-permute-start(f32[512,256]{1,0:T(8,128)} %constant_dynamic-update-slice_fusion.own), channel_id=1, source_target_pairs={{0,1},{1,0},{2,3},{3,2},{4,5},{5,4},{6,7},{7,6},{8,9},{9,8},{10,11... | collective-permute-start | bytes 1572872 | tf_op jit(solution)/shard_map/ppermute | solution.py:385
  64.5 5.5 %collective-permute-start.13 = (f32[512,256]{1,0:T(8,128)S(1)}, f32[512,256]{1,0:T(8,128)}, u32[]{:S(2)}, u32[]{:S(2)}) collective-permute-start(f32[512,256]{1,0:T(8,128)S(1)} %bitcast.60), channel_id=1, source_target_pairs={{0,1},{1,0},{2,3},{3,2},{4,5},{5,4},{6,7},{7,6},{8,9},{9,8},{10,11... | collective-permute-start | bytes 1572872 | tf_op jit(solution)/shard_map/ppermute | solution.py:385
  65.4 4.6 %copy-start.9 = (f32[16,96,256]{2,1,0:T(8,128)}, f32[16,96,256]{2,1,0:T(8,128)S(1)}, u32[]{:S(2)}) copy-start(f32[16,96,256]{2,1,0:T(8,128)S(1)} %all-to-all-done.cols) | copy-start | bytes 4718596
  66.4 17.7 %all-to-all-start.2 = ((f32[8,64,256]{2,1,0:T(8,128)}), f32[8,64,256]{2,1,0:T(8,128)S(1)}, u32[]{:S(2)}, u32[]{:S(2)}) async-start(f32[8,64,256]{2,1,0:T(8,128)} %broadcast_in_dim.20), calls=%async_computation.2 | async-start | bytes 1048576 | tf_op jit(solution)/shard_map/all_to_all | solution.py:434
  78.5 14.0 %collective-permute-start.14 = (f32[4,2,112,256]{3,2,1,0:T(8,128)}, f32[4,2,112,256]{3,2,1,0:T(8,128)}, u32[]{:S(2)}, u32[]{:S(2)}) collective-permute-start(f32[4,2,112,256]{3,2,1,0:T(8,128)} %get-tuple-element.55), channel_id=1, source_target_pairs={{0,1},{1,0},{2,3},{3,2},{4,5},{5,4},{6,7},{7,6},{8,9},{9,8},{10,11... | collective-permute-start | bytes 2752520 | tf_op jit(solution)/shard_map/ppermute | solution.py:385
  84.1 32.7 %all-to-all-start.1 = ((f32[16,88,256]{2,1,0:T(8,128)}), f32[16,88,256]{2,1,0:T(8,128)S(1)}, u32[]{:S(2)}, u32[]{:S(2)}) async-start(f32[16,88,256]{2,1,0:T(8,128)} %get-tuple-element.53), calls=%async_computation.1 | async-start | bytes 2883584 | tf_op jit(solution)/shard_map/all_to_all | solution.py:438
  92.6 11.1 %copy-start.8 = (s32[14]{0:T(128)S(1)}, s32[14]{0:T(128)}, u32[]{:S(2)}) copy-start(s32[14]{0:T(128)} %concatenate.36.info) | copy-start | bytes 172
  94.3 7.8 %collective-permute-start.18 = (f32[8,64,256]{2,1,0:T(8,128)S(1)}, f32[8,64,256]{2,1,0:T(8,128)S(1)}, u32[]{:S(2)}, u32[]{:S(2)}) collective-permute-start(f32[8,64,256]{2,1,0:T(8,128)S(1)} %all-to-all-done.2.own), channel_id=1, source_target_pairs={{0,1},{1,0},{2,3},{3,2},{4,5},{5,4},{6,7},{7,6},{8,9},{9,8},{10,11... | collective-permute-start | bytes 1572872 | tf_op jit(solution)/shard_map/ppermute | solution.py:385
  97.5 18.3 %collective-permute-start.15 = (f32[2,112,256]{2,1,0:T(8,128)S(1)}, f32[2,112,256]{2,1,0:T(8,128)S(1)}, u32[]{:S(2)}, u32[]{:S(2)}) collective-permute-start(f32[2,112,256]{2,1,0:T(8,128)S(1)} %get-tuple-element.57), channel_id=1, source_target_pairs={{0,2},{1,3},{2,0},{3,1},{4,6},{5,7},{6,4},{7,5},{8,10},{9,11},{10,... | collective-permute-start | bytes 688136 | tf_op jit(solution)/shard_map/ppermute | solution.py:385
  97.8 18.0 %collective-permute-start.16 = (f32[2,112,256]{2,1,0:T(8,128)S(1)}, f32[2,112,256]{2,1,0:T(8,128)S(1)}, u32[]{:S(2)}, u32[]{:S(2)}) collective-permute-start(f32[2,112,256]{2,1,0:T(8,128)S(1)} %get-tuple-element.58), channel_id=1, source_target_pairs={{0,4},{1,5},{2,6},{3,7},{4,0},{5,1},{6,2},{7,3},{8,12},{9,13},{10,... | collective-permute-start | bytes 688136 | tf_op jit(solution)/shard_map/ppermute | solution.py:385
  97.8 18.0 %collective-permute-start.17 = (f32[2,112,256]{2,1,0:T(8,128)S(1)}, f32[2,112,256]{2,1,0:T(8,128)S(1)}, u32[]{:S(2)}, u32[]{:S(2)}) collective-permute-start(f32[2,112,256]{2,1,0:T(8,128)S(1)} %get-tuple-element.59), channel_id=1, source_target_pairs={{0,6},{1,7},{2,4},{3,5},{4,2},{5,3},{6,0},{7,1},{8,14},{9,15},{10,... | collective-permute-start | bytes 688136 | tf_op jit(solution)/shard_map/ppermute | solution.py:385
  102.0 23.2 %copy-start.11 = (f32[256,256]{1,0:T(8,128)}, f32[256,256]{1,0:T(8,128)S(1)}, u32[]{:S(2)}) copy-start(f32[256,256]{1,0:T(8,128)S(1)} %slice_bitcast_fusion.1.edge) | copy-start | bytes 786436
  102.0 22.0 %collective-permute-start.21 = (f32[256,256]{1,0:T(8,128)S(1)}, f32[256,256]{1,0:T(8,128)S(1)}, u32[]{:S(2)}, u32[]{:S(2)}) collective-permute-start(f32[256,256]{1,0:T(8,128)S(1)} %slice_bitcast_fusion.1.edge), channel_id=1, source_target_pairs={{17,0}} | collective-permute-start | bytes 786440 | tf_op jit(solution)/shard_map/ppermute | solution.py:447
  102.7 21.3 %collective-permute-start.20 = (f32[256,256]{1,0:T(8,128)S(1)}, f32[256,256]{1,0:T(8,128)S(1)}, u32[]{:S(2)}, u32[]{:S(2)}) collective-permute-start(f32[256,256]{1,0:T(8,128)S(1)} %slice_bitcast_fusion.1.edge), channel_id=1, source_target_pairs={{16,0},{17,16}} | collective-permute-start | bytes 786440 | tf_op jit(solution)/shard_map/ppermute | solution.py:446
  115.7 0.7 copy-start.3
  115.8 43.6 %copy-start.1 = (f32[256,256]{1,0:T(8,128)}, f32[256,256]{1,0:T(8,128)S(1)}, u32[]{:S(2)}) copy-start(f32[256,256]{1,0:T(8,128)S(1)} %get-tuple-element.77.v0_ref.v0) | copy-start | bytes 786436
  115.8 43.6 %copy-start.2 = (f32[256,256]{1,0:T(8,128)}, f32[256,256]{1,0:T(8,128)S(1)}, u32[]{:S(2)}) copy-start(f32[256,256]{1,0:T(8,128)S(1)} %get-tuple-element.78.p_ref.p01) | copy-start | bytes 786436
  116.5 7.5 %collective-permute-start.19 = (f32[112,256]{1,0:T(8,128)S(1)}, f32[112,256]{1,0:T(8,128)S(1)}, u32[]{:S(2)}, u32[]{:S(2)}) collective-permute-start(f32[112,256]{1,0:T(8,128)S(1)} %get-tuple-element.127), channel_id=1, source_target_pairs={{0,8},{1,9},{2,10},{3,11},{4,12},{5,13},{6,14},{7,15},{8,0},{9,1},... | collective-permute-start | bytes 344072 | tf_op jit(solution)/shard_map/ppermute | solution.py:385
  124.0 41.0 %copy-start.14 = (f32[256,256]{1,0:T(8,128)}, f32[256,256]{1,0:T(8,128)S(1)}, u32[]{:S(2)}) copy-start(f32[256,256]{1,0:T(8,128)S(1)} %collective-permute-done.21.far_edge) | copy-start | bytes 786436
  124.0 41.0 %copy-start.15 = (f32[256,256]{1,0:T(8,128)}, f32[256,256]{1,0:T(8,128)S(1)}, u32[]{:S(2)}) copy-start(f32[256,256]{1,0:T(8,128)S(1)} %collective-permute-done.20.near_edge) | copy-start | bytes 786436
  125.2 41.2 %all-to-all-start.3 = ((f32[16,72,256]{2,1,0:T(8,128)}), f32[16,72,256]{2,1,0:T(8,128)S(1)}, u32[]{:S(2)}, u32[]{:S(2)}) async-start(f32[16,72,256]{2,1,0:T(8,128)} %get-tuple-element.72), calls=%async_computation.3 | async-start | bytes 2359296 | tf_op jit(solution)/shard_map/all_to_all | solution.py:454
  131.9 34.6 %collective-permute-start.22 = (f32[64,256]{1,0:T(8,128)S(1)}, f32[64,256]{1,0:T(8,128)S(1)}, u32[]{:S(2)}, u32[]{:S(2)}) collective-permute-start(f32[64,256]{1,0:T(8,128)S(1)} %get-tuple-element.73), channel_id=1, source_target_pairs={{0,0},{1,16},{2,32},{3,48},{4,64},{5,80},{6,96},{7,112},{8,128},{9... | collective-permute-start | bytes 196616 | tf_op jit(solution)/shard_map/ppermute | solution.py:389
  165.1 0.7 copy-start.4
  165.8 0.7 copy-start.5
  166.5 6.6 %copy-start.6 = (f32[256,256]{1,0:T(8,128)}, f32[256,256]{1,0:T(8,128)S(1)}, u32[]{:S(2)}) copy-start(f32[256,256]{1,0:T(8,128)S(1)} %get-tuple-element.90.u) | copy-start | bytes 786436
  166.5 28.3 %copy-start.7 = (f32[384,256]{1,0:T(8,128)}, f32[384,256]{1,0:T(8,128)S(1)}, u32[]{:S(2)}) copy-start(f32[384,256]{1,0:T(8,128)S(1)} %get-tuple-element.95.d_own) | copy-start | bytes 1179652
  166.6 17.3 %collective-permute-start.29 = (f32[112,256]{1,0:T(8,128)S(1)}, f32[112,256]{1,0:T(8,128)S(1)}, u32[]{:S(2)}, u32[]{:S(2)}) collective-permute-start(f32[112,256]{1,0:T(8,128)S(1)} %get-tuple-element.94.refs_0_), channel_id=1, source_target_pairs={{14,0},{15,1},{30,16},{31,17},{46,32},{47,33},{62,48},{63,49},{78,... | collective-permute-start | bytes 344072 | tf_op jit(solution)/shard_map/ppermute | solution.py:464
  167.9 17.3 %collective-permute-start.28 = (f32[112,256]{1,0:T(8,128)S(1)}, f32[112,256]{1,0:T(8,128)S(1)}, u32[]{:S(2)}, u32[]{:S(2)}) collective-permute-start(f32[112,256]{1,0:T(8,128)S(1)} %get-tuple-element.94.refs_0_), channel_id=1, source_target_pairs={{12,0},{13,1},{28,16},{29,17},{44,32},{45,33},{60,48},{61,49},{76,... | collective-permute-start | bytes 344072 | tf_op jit(solution)/shard_map/ppermute | solution.py:464
  169.2 17.3 %collective-permute-start.27 = (f32[112,256]{1,0:T(8,128)S(1)}, f32[112,256]{1,0:T(8,128)S(1)}, u32[]{:S(2)}, u32[]{:S(2)}) collective-permute-start(f32[112,256]{1,0:T(8,128)S(1)} %get-tuple-element.94.refs_0_), channel_id=1, source_target_pairs={{10,0},{11,1},{26,16},{27,17},{42,32},{43,33},{58,48},{59,49},{74,... | collective-permute-start | bytes 344072 | tf_op jit(solution)/shard_map/ppermute | solution.py:464
  170.5 16.0 %collective-permute-start.26 = (f32[112,256]{1,0:T(8,128)S(1)}, f32[112,256]{1,0:T(8,128)S(1)}, u32[]{:S(2)}, u32[]{:S(2)}) collective-permute-start(f32[112,256]{1,0:T(8,128)S(1)} %get-tuple-element.94.refs_0_), channel_id=1, source_target_pairs={{8,0},{9,1},{24,16},{25,17},{40,32},{41,33},{56,48},{57,49},{72,64... | collective-permute-start | bytes 344072 | tf_op jit(solution)/shard_map/ppermute | solution.py:464
  171.8 14.8 %collective-permute-start.25 = (f32[112,256]{1,0:T(8,128)S(1)}, f32[112,256]{1,0:T(8,128)S(1)}, u32[]{:S(2)}, u32[]{:S(2)}) collective-permute-start(f32[112,256]{1,0:T(8,128)S(1)} %get-tuple-element.94.refs_0_), channel_id=1, source_target_pairs={{6,0},{7,1},{22,16},{23,17},{38,32},{39,33},{54,48},{55,49},{70,64... | collective-permute-start | bytes 344072 | tf_op jit(solution)/shard_map/ppermute | solution.py:464
  183.9 7.0 %collective-permute-start.24 = (f32[112,256]{1,0:T(8,128)S(1)}, f32[112,256]{1,0:T(8,128)S(1)}, u32[]{:S(2)}, u32[]{:S(2)}) collective-permute-start(f32[112,256]{1,0:T(8,128)S(1)} %get-tuple-element.94.refs_0_), channel_id=1, source_target_pairs={{4,0},{5,1},{20,16},{21,17},{36,32},{37,33},{52,48},{53,49},{68,64... | collective-permute-start | bytes 344072 | tf_op jit(solution)/shard_map/ppermute | solution.py:464
  185.2 9.0 %collective-permute-start.23 = (f32[112,256]{1,0:T(8,128)S(1)}, f32[112,256]{1,0:T(8,128)S(1)}, u32[]{:S(2)}, u32[]{:S(2)}) collective-permute-start(f32[112,256]{1,0:T(8,128)S(1)} %get-tuple-element.94.refs_0_), channel_id=1, source_target_pairs={{2,0},{3,1},{18,16},{19,17},{34,32},{35,33},{50,48},{51,49},{66,64... | collective-permute-start | bytes 344072 | tf_op jit(solution)/shard_map/ppermute | solution.py:464
  194.3 3.3 %copy-start = (f32[896,256]{1,0:T(8,128)}, f32[896,256]{1,0:T(8,128)S(1)}, u32[]{:S(2)}) copy-start(f32[896,256]{1,0:T(8,128)S(1)} %joined.1.mine) | copy-start | bytes 2752516
  194.3 3.2 %collective-permute-start.30 = (f32[896,256]{1,0:T(8,128)S(1)}, f32[896,256]{1,0:T(8,128)S(1)}, u32[]{:S(2)}, u32[]{:S(2)}) collective-permute-start(f32[896,256]{1,0:T(8,128)S(1)} %joined.1.mine), channel_id=1, source_target_pairs={{0,1},{1,0},{2,3},{3,2},{4,5},{5,4},{6,7},{7,6},{8,9},{9,8},{10,11... | collective-permute-start | bytes 2752520 | tf_op jit(solution)/shard_map/ppermute | solution.py:385
  194.9 2.7 %collective-permute-start.31 = (f32[384,256]{1,0:T(8,128)S(1)}, f32[384,256]{1,0:T(8,128)S(1)}, u32[]{:S(2)}, u32[]{:S(2)}) collective-permute-start(f32[384,256]{1,0:T(8,128)S(1)} %get-tuple-element.95.d_own), channel_id=1, source_target_pairs={{0,1},{1,0},{2,3},{3,2},{4,5},{5,4},{6,7},{7,6},{8,9},{9,8},{10,11... | collective-permute-start | bytes 1179656 | tf_op jit(solution)/shard_map/ppermute | solution.py:385
  197.5 0.7 copy-start.13
  198.3 0.9 copy-start.12
